TPU v7x, 256 devices: a whole 4x4x8 slice. The times are simulated.
256 devices in a mesh: dp: 4 (over x), gx: 2 (over core), yz: 32 (over z, y).
Axes of the slice: x: 4, y: 4, z: 8, core: 2. Of those that a mesh axis runs over, the one named last changes fastest.
Arguments:
- volumes: bfloat16 [4, 4, 2, 32, 16384], P('dp', None, 'gx', 'yz'), may hold values from -6 to 6
- first_kernel: bfloat16 [32, 4, 3, 3, 3], replicated, may hold values from -0.625 to 0.625
- second_kernel: bfloat16 [64, 32, 3, 3, 3], replicated, may hold values from -0.21875 to 0.21875
- cotangent: bfloat16 [4, 64, 2, 32, 256], P('dp', None, 'gx', 'yz'), may hold values from -6 to 6
Outputs:
- features: bfloat16 [4, 64, 2, 32, 256], P('dp', None, 'gx', 'yz')
- act_grad: float32 [4, 32, 2, 32, 2048], P('dp', None, 'gx', 'yz')
- first_grad: float32 [32, 4, 3, 3, 3], replicated
- second_grad: float32 [64, 32, 3, 3, 3], replicated
All inputs are finite; a program needn't handle non-finite values.
Results may differ from a plain program's by a relative error of at most 0.019.
The roundings to bfloat16 on the way count: a program that leaves them out, or rounds other values in their place, can miss the bound.
Values may be sent and summed in bfloat16 or wider, within the bound.
A program may use at most 128 MiB of HBM per device.

v0:
```python
import jax
import jax.numpy as jnp
from jax import lax
from jax.sharding import PartitionSpec as P

CX = 32
CY = 32
CZ = 16


SLOPE = 0.3


def passed_along(block, axis, distance):
    devices = range(lax.axis_size(axis))
    route = [(i - distance, i) for i in devices if i - distance in devices]
    return lax.ppermute(block, axis, route)


def convolve_valid(padded, kernel):
    return lax.conv_general_dilated(
        padded,
        kernel,
        (1, 1, 1),
        "VALID",
        dimension_numbers=("NCDHW", "OIDHW", "NCDHW"),
        preferred_element_type=jnp.float32,
    )


def kernel_grad(padded, grad):
    result = lax.conv_general_dilated(
        padded,
        grad,
        (1, 1, 1),
        "VALID",
        dimension_numbers=("CNDHW", "IODHW", "NCDHW"),
        preferred_element_type=jnp.float32,
    )
    return result.transpose(1, 0, 2, 3, 4)


def leaky(values):
    return jnp.where(values > 0, values, SLOPE * values)


def leaky_slope(values):
    return jnp.where(values > 0, jnp.float32(1.0), jnp.float32(SLOPE))


def average_pool(values):
    bat, chan, xs, ys, zs = values.shape
    return values.reshape(bat, chan, xs // 2, 2, ys // 2, 2, zs // 2, 2).mean(axis=(3, 5, 7))


def spread_back(values):
    bat, chan, xs, ys, zs = values.shape
    grown = jnp.broadcast_to(
        values[:, :, :, None, :, None, :, None], (bat, chan, xs, 2, ys, 2, zs, 2)
    )
    return grown.reshape(bat, chan, 2 * xs, 2 * ys, 2 * zs) * 0.125


def unflatten(values, factor):
    return values[:, :, 0, 0].reshape(
        values.shape[0], values.shape[1], CX // factor, CY // factor, CZ // factor
    )


def flatten(values):
    return values.reshape(values.shape[0], values.shape[1], 1, 1, -1)


def block_coords():
    count = lax.axis_size("yz")
    rows_y = min(4, count)
    rows_z = count // rows_y
    place = lax.axis_index("yz")
    return (count, rows_y, rows_z, place // rows_z, place % rows_z)


def inside(offset, where, limit):
    return jnp.logical_and(where + offset >= 0, where + offset < limit)


def send_range(offset, length):
    if offset == 1:
        return (0, 1)
    if offset == -1:
        return (length - 1, length)
    return (0, length)


def put_range(offset, length):
    if offset == 1:
        return (length + 1, length + 2)
    if offset == -1:
        return (0, 1)
    return (1, length + 1)


def extend(values):
    count, rows_y, rows_z, block_y, block_z = block_coords()
    plane = lax.axis_index("gx")
    planes = lax.axis_size("gx")
    sizes = values.shape[2:]
    grown = jnp.pad(values, ((0, 0), (0, 0), (1, 1), (1, 1), (1, 1)))
    for step_x in (-1, 0, 1):
        for step_y in (-1, 0, 1):
            for step_z in (-1, 0, 1):
                if step_x == 0 and step_y == 0 and (step_z == 0):
                    continue
                steps = (step_x, step_y, step_z)
                low = [send_range(steps[k], sizes[k]) for k in range(3)]
                high = [put_range(steps[k], sizes[k]) for k in range(3)]
                piece = values[
                    :, :, low[0][0] : low[0][1], low[1][0] : low[1][1], low[2][0] : low[2][1]
                ]
                moved = -(step_x * count + step_y * rows_z + step_z)
                got = passed_along(piece, ("gx", "yz"), moved)
                valid = jnp.logical_and(
                    inside(step_x, plane, planes),
                    jnp.logical_and(
                        inside(step_y, block_y, rows_y), inside(step_z, block_z, rows_z)
                    ),
                )
                got = got * valid.astype(got.dtype)
                grown = grown.at[
                    :, :, high[0][0] : high[0][1], high[1][0] : high[1][1], high[2][0] : high[2][1]
                ].set(got)
    return grown


def on_device(volumes, first_kernel, second_kernel, cotangent):
    local_in = unflatten(volumes, 1)
    upstream = unflatten(cotangent, 4)
    padded_in = extend(local_in)
    pre_first = convolve_valid(padded_in, first_kernel)
    act_first = average_pool(leaky(pre_first)).astype(jnp.bfloat16)
    padded_mid = extend(act_first)
    pre_second = convolve_valid(padded_mid, second_kernel)
    features = average_pool(leaky(pre_second)).astype(jnp.bfloat16)
    grad_second = (spread_back(upstream.astype(jnp.float32)) * leaky_slope(pre_second)).astype(
        jnp.bfloat16
    )
    flipped = jnp.flip(second_kernel, (2, 3, 4)).transpose(1, 0, 2, 3, 4)
    act_grad = convolve_valid(extend(grad_second), flipped)
    grad_first = (spread_back(act_grad) * leaky_slope(pre_first)).astype(jnp.bfloat16)
    first_grad, second_grad = lax.psum(
        (kernel_grad(padded_in, grad_first), kernel_grad(padded_mid, grad_second)),
        ("dp", "gx", "yz"),
    )
    return (flatten(features), flatten(act_grad), first_grad, second_grad)


def solution(mesh):
    placed = (P("dp", None, "gx", "yz", None), P(), P(), P("dp", None, "gx", "yz", None))
    return jax.shard_map(
        on_device,
        mesh=mesh,
        in_specs=placed,
        out_specs=(P("dp", None, "gx", "yz", None), P("dp", None, "gx", "yz", None), P(), P()),
        check_vma=False,
    )
```

profile of v0, /device:TPU:1, one launch (start us, length us, event | category | flops | bytes accessed | tf_op | source)
XLA Modules:
  0.0 856.8 jit_solution(7753075916241822613)
XLA Ops:
  21.2 13.3 %collective-permute-start.5 = (bf16[1,4,1,32,1]{4,3,2,1,0:T(8,128)(2,1)}, bf16[1,4,1,32,1]{4,3,2,1,0:T(8,128)(2,1)S(1)}, u32[]{:S(2)}, u32[]{:S(2)}) collective-permute-start(bf16[1,4,1,32,1]{4,3,2,1,0:T(8,128)(2,1)} %get-tuple-element.1002), channel_id=1, source_target_pairs={{0,31},{1,32},{2,33},{3,34},{4,35},{5,36},{6,37},{7,38},{8,39},{9,... | collective-permute-start | bytes 776 | tf_op jit(solution)/shard_map/ppermute | solution.py:17
  50.2 7.5 collective-permute-done.17
  66.9 11.7 %collective-permute-start.7 = (bf16[1,4,1,1,16]{4,3,2,1,0:T(2,128)(2,1)S(1)}, bf16[1,4,1,1,16]{4,3,2,1,0:T(2,128)(2,1)S(1)}, u32[]{:S(2)}, u32[]{:S(2)}) collective-permute-start(bf16[1,4,1,1,16]{4,3,2,1,0:T(2,128)(2,1)S(1)} %get-tuple-element.998), channel_id=1, source_target_pairs={{0,24},{1,25},{2,26},{3,27},{4,28},{5,29},{6,30},{7,31},{8,32},{9,... | collective-permute-start | bytes 392 | tf_op jit(solution)/shard_map/ppermute | solution.py:17
  113.9 9.6 %collective-permute-start.16 = (bf16[1,4,32,1,1]{4,3,2,1,0:T(2,128)(2,1)S(1)}, bf16[1,4,32,1,1]{4,3,2,1,0:T(2,128)(2,1)S(1)}, u32[]{:S(2)}, u32[]{:S(2)}) collective-permute-start(bf16[1,4,32,1,1]{4,3,2,1,0:T(2,128)(2,1)S(1)} %get-tuple-element.1006), channel_id=1, source_target_pairs={{9,0},{10,1},{11,2},{12,3},{13,4},{14,5},{15,6},{16,7},{17,8},{18,... | collective-permute-start | bytes 776 | tf_op jit(solution)/shard_map/ppermute | solution.py:17
  126.8 8.3 collective-permute-start.13
  144.0 9.3 %collective-permute-start.15 = (bf16[1,4,32,1,16]{4,3,2,1,0:T(2,128)(2,1)S(1)}, bf16[1,4,32,1,16]{4,3,2,1,0:T(2,128)(2,1)S(1)}, u32[]{:S(2)}, u32[]{:S(2)}) collective-permute-start(bf16[1,4,32,1,16]{4,3,2,1,0:T(2,128)(2,1)S(1)} %get-tuple-element.1010), channel_id=1, source_target_pairs={{8,0},{9,1},{10,2},{11,3},{12,4},{13,5},{14,6},{15,7},{16,8},{17,9... | collective-permute-start | bytes 12296 | tf_op jit(solution)/shard_map/ppermute | solution.py:17
  162.2 21.7 %scatter.276 = bf16[1,4,34,34,18]{4,3,2,1,0:T(8,128)(2,1)S(1)} dynamic-update-slice(bf16[1,4,34,34,18]{4,3,2,1,0:T(8,128)(2,1)S(1)} %scatter.275, bf16[1,4,32,1,16]{4,3,2,1,0:T(2,128)(2,1)S(1)} %broadcast_multiply_fusion.7, s32[]{:T(128)} %constant.2253.clone.1, s32[]{:T(128)} %constant.2253.clone.1, s32[]{:T(128)} %constant.2256.clone.1, s32[]{:T(128)} %constant.2253.clone.1, s32[]{:T(128)} %constant.2256.clone.1) | dynamic-update-slice | bytes 8196 | tf_op jit(solution)/shard_map/scatter | solution.py:130
  183.9 10.9 %scatter.279 = bf16[1,4,34,34,18]{4,3,2,1,0:T(8,128)(2,1)S(1)} dynamic-update-slice(bf16[1,4,34,34,18]{4,3,2,1,0:T(8,128)(2,1)S(1)} %scatter.276, bf16[1,4,32,1,1]{4,3,2,1,0:T(2,128)(2,1)S(1)} %broadcast_multiply_fusion.6, s32[]{:T(128)} %constant.2253.clone.1, s32[]{:T(128)} %constant.2253.clone.1, s32[]{:T(128)} %constant.2256.clone.1, s32[]{:T(128)} %constant.2253.clone.1, s32[]{:T(128)} %constant.2261.clone.1) | dynamic-update-slice | bytes 516 | tf_op jit(solution)/shard_map/scatter | solution.py:130
  198.3 7.8 scatter.280
  206.1 27.2 %scatter.281 = bf16[1,4,34,34,18]{4,3,2,1,0:T(8,128)(2,1)S(1)} dynamic-update-slice(bf16[1,4,34,34,18]{4,3,2,1,0:T(8,128)(2,1)S(1)} %scatter.280, bf16[1,4,32,32,1]{4,3,2,1,0:T(8,128)(2,1)} %copy.94, s32[]{:T(128)} %constant.2253.clone.1, s32[]{:T(128)} %constant.2253.clone.1, s32[]{:T(128)} %constant.2256.clone.1, s32[]{:T(128)} %constant.2256.clone.1, s32[]{:T(128)} %constant.2261.clone.1) | dynamic-update-slice | bytes 16388 | tf_op jit(solution)/shard_map/scatter | solution.py:130
  235.7 21.7 %scatter.285 = bf16[1,4,34,34,18]{4,3,2,1,0:T(8,128)(2,1)S(1)} dynamic-update-slice(bf16[1,4,34,34,18]{4,3,2,1,0:T(8,128)(2,1)S(1)} %scatter.284, bf16[1,4,32,1,16]{4,3,2,1,0:T(2,128)(2,1)S(1)} %broadcast_multiply_fusion.4, s32[]{:T(128)} %constant.2253.clone.1, s32[]{:T(128)} %constant.2253.clone.1, s32[]{:T(128)} %constant.2256.clone.1, s32[]{:T(128)} %constant.2262.clone.1, s32[]{:T(128)} %constant.2256.clone.1) | dynamic-update-slice | bytes 8196 | tf_op jit(solution)/shard_map/scatter | solution.py:130
  257.4 10.9 %scatter.286 = bf16[1,4,34,34,18]{4,3,2,1,0:T(8,128)(2,1)S(1)} dynamic-update-slice(bf16[1,4,34,34,18]{4,3,2,1,0:T(8,128)(2,1)S(1)} %scatter.285, bf16[1,4,32,1,1]{4,3,2,1,0:T(2,128)(2,1)S(1)} %broadcast_multiply_fusion.3, s32[]{:T(128)} %constant.2253.clone.1, s32[]{:T(128)} %constant.2253.clone.1, s32[]{:T(128)} %constant.2256.clone.1, s32[]{:T(128)} %constant.2262.clone.1, s32[]{:T(128)} %constant.2261.clone.1) | dynamic-update-slice | bytes 516 | tf_op jit(solution)/shard_map/scatter | solution.py:130
  283.6 30.6 %compare_select_fusion = (f32[32,32,8,3,32]{4,2,3,1,0:T(8,128)}, f32[32,32,8,3,32]{4,2,3,1,0:T(8,128)}) fusion(pred[8,3]{0,1:T(4,128)(4,1)S(1)} %copy-done.13, bf16[32,4,3,3,3]{0,1,4,3,2:T(4,128)(2,1)S(1)} %copy-done.12, bf16[4,34,34,1,7,2]{4,0,5,2,1,3:T(4,128)(2,1)S(1)} %slice.3569, bf16[4,34,34,1,8,3]{4,0,5,2,1,3:T(4,128)(2,1)S(1)} %copy-done.2), kind=kOutput, calls=%fused_computation.1 | convolution fusion | flops 174911232 | bytes 6649816 | tf_op jit(solution)/shard_map/conv_general_dilated | solution.py:21
  314.2 11.4 %copy.98 = f32[32,32,8,3,32]{4,1,3,2,0:T(8,128)} copy(f32[32,32,8,3,32]{4,2,3,1,0:T(8,128)} %get-tuple-element.961) | data formatting | bytes 6291456 | tf_op jit(solution)/shard_map/jit(_where)/select_n | solution.py:44
  325.6 8.3 slice.3570
  333.9 9.6 %reduce_sum.18 = f32[32,16,16,8]{0,2,3,1:T(8,128)S(1)} reduce(f32[32,16,2,16,2,8,2]{0,4,3,6,5,2,1:T(2,128)} %bitcast.39, f32[]{:T(128)} %constant.2263.clone.1), dimensions={2,4,6}, to_apply=%region_0.1 | reduce | flops 458752 | bytes 2359300 | tf_op jit(solution)/shard_map/reduce_sum | solution.py:53
  345.5 21.8 %copy.104 = bf16[1,4,34,34,18]{1,0,4,3,2:T(2,128)(2,1)} copy(bf16[1,4,34,34,18]{4,3,2,1,0:T(8,128)(2,1)S(1)} %scatter.301) | data formatting | bytes 332928 | tf_op jit(solution)/shard_map/scatter | solution.py:130
  371.5 11.5 %copy.103 = f32[32,32,8,3,32]{4,1,3,2,0:T(8,128)} copy(f32[32,32,8,3,32]{4,2,3,1,0:T(8,128)} %get-tuple-element.960) | data formatting | bytes 6291456 | tf_op jit(solution)/shard_map/jit(_where)/select_n | solution.py:48
  406.5 7.4 collective-permute-done.43
  422.6 16.0 %collective-permute-start.33 = (bf16[1,32,1,1,8]{1,4,3,2,0:T(8,128)(2,1)S(1)}, bf16[1,32,1,1,8]{1,4,3,2,0:T(8,128)(2,1)S(1)}, u32[]{:S(2)}, u32[]{:S(2)}) collective-permute-start(bf16[1,32,1,1,8]{1,4,3,2,0:T(8,128)(2,1)S(1)} %get-tuple-element.1024), channel_id=1, source_target_pairs={{0,24},{1,25},{2,26},{3,27},{4,28},{5,29},{6,30},{7,31},{8,32},{9,... | collective-permute-start | bytes 1544 | tf_op jit(solution)/shard_map/ppermute | solution.py:17
  463.5 7.0 collective-permute-start.39
  492.0 9.0 %collective-permute-start.41 = (bf16[1,32,16,1,8]{1,4,3,2,0:T(8,128)(2,1)S(1)}, bf16[1,32,16,1,8]{1,4,3,2,0:T(8,128)(2,1)S(1)}, u32[]{:S(2)}, u32[]{:S(2)}) collective-permute-start(bf16[1,32,16,1,8]{1,4,3,2,0:T(8,128)(2,1)S(1)} %get-tuple-element.1036), channel_id=1, source_target_pairs={{8,0},{9,1},{10,2},{11,3},{12,4},{13,5},{14,6},{15,7},{16,8},{17,9... | collective-permute-start | bytes 24584 | tf_op jit(solution)/shard_map/ppermute | solution.py:17
  511.0 9.5 %fusion.17 = (u16[1,64,16,8]{1,0,3,2:T(2,128)(2,1)S(1)}, f32[1,64,16,16,8]{1,0,4,3,2:T(1,128)S(1)}) fusion(bf16[64,32,3,3,3]{0,1,4,3,2:T(8,128)(2,1)S(1)} %copy-done, bf16[1,32,18,18,10]{1,4,3,2,0:T(8,128)(2,1)S(1)} %scatter.345), kind=kOutput, calls=%fused_computation.25 | convolution fusion | flops 227139584 | bytes 858624 | tf_op jit(solution)/shard_map/conv_general_dilated | solution.py:21
  524.7 12.2 %fusion.18 = f32[64,32,3,3,3]{0,1,4,3,2:T(8,128)} fusion(bf16[1,64,16,16,8]{1,0,4,3,2:T(2,128)(2,1)S(1)} %get-tuple-element.1040, bf16[1,32,18,18,10]{1,4,3,2,0:T(8,128)(2,1)S(1)} %scatter.345), kind=kOutput, calls=%fused_computation.26 | convolution fusion | flops 226492416 | bytes 690688 | tf_op jit(solution)/shard_map/transpose | solution.py:40
  546.0 9.6 %collective-permute-start.57 = (bf16[1,64,1,16,1]{1,0,4,3,2:T(2,128)(2,1)S(1)}, bf16[1,64,1,16,1]{1,0,4,3,2:T(2,128)(2,1)S(1)}, u32[]{:S(2)}, u32[]{:S(2)}) collective-permute-start(bf16[1,64,1,16,1]{1,0,4,3,2:T(2,128)(2,1)S(1)} %get-tuple-element.976), channel_id=1, source_target_pairs={{0,31},{1,32},{2,33},{3,34},{4,35},{5,36},{6,37},{7,38},{8,39},{9,... | collective-permute-start | bytes 6152 | tf_op jit(solution)/shard_map/ppermute | solution.py:17
  578.1 7.0 collective-permute-start.65
  594.0 10.8 %collective-permute-start.68 = (bf16[1,64,16,1,1]{1,0,4,3,2:T(2,128)(2,1)S(1)}, bf16[1,64,16,1,1]{1,0,4,3,2:T(2,128)(2,1)S(1)}, u32[]{:S(2)}, u32[]{:S(2)}) collective-permute-start(bf16[1,64,16,1,1]{1,0,4,3,2:T(2,128)(2,1)S(1)} %get-tuple-element.980), channel_id=1, source_target_pairs={{9,0},{10,1},{11,2},{12,3},{13,4},{14,5},{15,6},{16,7},{17,8},{18,... | collective-permute-start | bytes 6152 | tf_op jit(solution)/shard_map/ppermute | solution.py:17
  625.9 24.5 %broadcast_multiply_fusion = (f32[1,32,16,16,8]{1,0,4,3,2:T(1,128)S(1)}, f32[1,32,16,16,8]{1,0,4,3,2:T(1,128)}) fusion(bf16[1,64,18,18,10]{1,0,4,3,2:T(2,128)(2,1)} %constant_dynamic-update-slice_fusion, bf16[64,32,3,3,3]{0,1,4,3,2:T(8,128)(2,1)S(1)} %copy-done), kind=kOutput, calls=%fused_computation.31 | convolution fusion | flops 226557952 | bytes 1049600 | tf_op jit(solution)/shard_map/conv_general_dilated | solution.py:21
  650.6 7.6 broadcast_in_dim.26
  658.2 8.0 fusion.2
  666.2 100.1 %fusion.3 = f32[32,4,3,3,3]{0,1,4,3,2:T(4,128)S(1)} fusion(bf16[1,4,34,34,18]{1,0,4,3,2:T(2,128)(2,1)} %copy.104, bf16[1,32,32,32,16]{1,3,4,2,0:T(8,128)(2,1)S(1)} %fusion.2), kind=kOutput, calls=%fused_computation.7 | convolution fusion | flops 113246208 | bytes 1228864 | tf_op jit(solution)/shard_map/transpose | solution.py:40
  767.3 80.5 %psum.14 = f32[32,4,3,3,3]{0,1,4,3,2:T(4,128)} all-reduce(f32[32,4,3,3,3]{0,1,4,3,2:T(4,128)S(1)} %fusion.3), channel_id=1, replica_groups=mesh['dp'=4,'gx'=2,'yz'=32] {'dp','gx','yz'}, use_global_device_ids=true, to_apply=%region_2.3 | all-reduce | flops 3456 | bytes 27648 | tf_op jit(solution)/shard_map/psum | solution.py:149
  (343 shorter events, 278.1 us)
Async XLA Ops:
  7.2 840.6 %all-reduce.5.cloned.1.call-start = ((), (), s32[]{:S(2)}) async-start(), calls=%async_computation | async-start | bytes 884736 | tf_op jit(solution)/shard_map/psum | solution.py:149
  9.7 69.6 %collective-permute-start.1 = (bf16[1,4,1,1,16]{4,3,2,1,0:T(2,128)(2,1)S(1)}, bf16[1,4,1,1,16]{4,3,2,1,0:T(2,128)(2,1)S(1)}, u32[]{:S(2)}, u32[]{:S(2)}) collective-permute-start(bf16[1,4,1,1,16]{4,3,2,1,0:T(2,128)(2,1)S(1)} %get-tuple-element.999), channel_id=1, source_target_pairs={{0,40},{1,41},{2,42},{3,43},{4,44},{5,45},{6,46},{7,47},{8,48},{9,... | collective-permute-start | bytes 392 | tf_op jit(solution)/shard_map/ppermute | solution.py:17
  10.4 24.1 %collective-permute-start.2 = (bf16[1,4,1,1,1]{4,3,2,1,0:T(2,128)(2,1)S(1)}, bf16[1,4,1,1,1]{4,3,2,1,0:T(2,128)(2,1)S(1)}, u32[]{:S(2)}, u32[]{:S(2)}) collective-permute-start(bf16[1,4,1,1,1]{4,3,2,1,0:T(2,128)(2,1)S(1)} %get-tuple-element.994), channel_id=1, source_target_pairs={{0,39},{1,40},{2,41},{3,42},{4,43},{5,44},{6,45},{7,46},{8,47},{9,... | collective-permute-start | bytes 32 | tf_op jit(solution)/shard_map/ppermute | solution.py:17
  11.8 115.0 %collective-permute-start.3 = (bf16[1,4,1,32,1]{4,3,2,1,0:T(8,128)(2,1)S(1)}, bf16[1,4,1,32,1]{4,3,2,1,0:T(8,128)(2,1)S(1)}, u32[]{:S(2)}, u32[]{:S(2)}) collective-permute-start(bf16[1,4,1,32,1]{4,3,2,1,0:T(8,128)(2,1)S(1)} %get-tuple-element.1003), channel_id=1, source_target_pairs={{0,33},{1,34},{2,35},{3,36},{4,37},{5,38},{6,39},{7,40},{8,41},{9,... | collective-permute-start | bytes 776 | tf_op jit(solution)/shard_map/ppermute | solution.py:17
  13.0 142.0 %collective-permute-start.4 = (bf16[1,4,1,32,16]{4,3,2,1,0:T(8,128)(2,1)}, bf16[1,4,1,32,16]{4,3,2,1,0:T(8,128)(2,1)}, u32[]{:S(2)}, u32[]{:S(2)}) collective-permute-start(bf16[1,4,1,32,16]{4,3,2,1,0:T(8,128)(2,1)} %get-tuple-element.1005), channel_id=1, source_target_pairs={{0,32},{1,33},{2,34},{3,35},{4,36},{5,37},{6,38},{7,39},{8,40},{9,... | collective-permute-start | bytes 12296 | tf_op jit(solution)/shard_map/ppermute | solution.py:17
  21.2 113.9 %collective-permute-start.5 = (bf16[1,4,1,32,1]{4,3,2,1,0:T(8,128)(2,1)}, bf16[1,4,1,32,1]{4,3,2,1,0:T(8,128)(2,1)S(1)}, u32[]{:S(2)}, u32[]{:S(2)}) collective-permute-start(bf16[1,4,1,32,1]{4,3,2,1,0:T(8,128)(2,1)} %get-tuple-element.1002), channel_id=1, source_target_pairs={{0,31},{1,32},{2,33},{3,34},{4,35},{5,36},{6,37},{7,38},{8,39},{9,... | collective-permute-start | bytes 776 | tf_op jit(solution)/shard_map/ppermute | solution.py:17
  66.9 18.2 %collective-permute-start.7 = (bf16[1,4,1,1,16]{4,3,2,1,0:T(2,128)(2,1)S(1)}, bf16[1,4,1,1,16]{4,3,2,1,0:T(2,128)(2,1)S(1)}, u32[]{:S(2)}, u32[]{:S(2)}) collective-permute-start(bf16[1,4,1,1,16]{4,3,2,1,0:T(2,128)(2,1)S(1)} %get-tuple-element.998), channel_id=1, source_target_pairs={{0,24},{1,25},{2,26},{3,27},{4,28},{5,29},{6,30},{7,31},{8,32},{9,... | collective-permute-start | bytes 392 | tf_op jit(solution)/shard_map/ppermute | solution.py:17
  79.3 18.9 %collective-permute-start.9 = (bf16[1,4,32,1,1]{4,3,2,1,0:T(2,128)(2,1)S(1)}, bf16[1,4,32,1,1]{4,3,2,1,0:T(2,128)(2,1)S(1)}, u32[]{:S(2)}, u32[]{:S(2)}) collective-permute-start(bf16[1,4,32,1,1]{4,3,2,1,0:T(2,128)(2,1)S(1)} %get-tuple-element.1009), channel_id=1, source_target_pairs={{0,9},{1,10},{2,11},{3,12},{4,13},{5,14},{6,15},{7,16},{8,17},{9,1... | collective-permute-start | bytes 776 | tf_op jit(solution)/shard_map/ppermute | solution.py:17
  92.7 60.8 %collective-permute-start.10 = (bf16[1,4,32,1,16]{4,3,2,1,0:T(2,128)(2,1)S(1)}, bf16[1,4,32,1,16]{4,3,2,1,0:T(2,128)(2,1)S(1)}, u32[]{:S(2)}, u32[]{:S(2)}) collective-permute-start(bf16[1,4,32,1,16]{4,3,2,1,0:T(2,128)(2,1)S(1)} %get-tuple-element.1011), channel_id=1, source_target_pairs={{0,8},{1,9},{2,10},{3,11},{4,12},{5,13},{6,14},{7,15},{8,16},{9,17... | collective-permute-start | bytes 12296 | tf_op jit(solution)/shard_map/ppermute | solution.py:17
  124.8 70.0 %collective-permute-start.12 = (bf16[1,4,32,32,1]{3,2,4,1,0:T(8,128)(2,1)}, bf16[1,4,32,32,1]{3,2,4,1,0:T(8,128)(2,1)S(1)}, u32[]{:S(2)}, u32[]{:S(2)}) collective-permute-start(bf16[1,4,32,32,1]{3,2,4,1,0:T(8,128)(2,1)} %copy.91), channel_id=1, source_target_pairs={{0,1},{1,2},{2,3},{3,4},{4,5},{5,6},{6,7},{7,8},{8,9},{9,10},{10,1... | collective-permute-start | bytes 24584 | tf_op jit(solution)/shard_map/ppermute | solution.py:17
  126.8 68.9 %collective-permute-start.13 = (bf16[1,4,32,32,1]{3,2,4,1,0:T(8,128)(2,1)S(1)}, bf16[1,4,32,32,1]{3,2,4,1,0:T(8,128)(2,1)}, u32[]{:S(2)}, u32[]{:S(2)}) collective-permute-start(bf16[1,4,32,32,1]{3,2,4,1,0:T(8,128)(2,1)S(1)} %copy.93), channel_id=1, source_target_pairs={{1,0},{2,1},{3,2},{4,3},{5,4},{6,5},{7,6},{8,7},{9,8},{10,9},{11,1... | collective-permute-start | bytes 24584 | tf_op jit(solution)/shard_map/ppermute | solution.py:17
  367.9 70.7 %collective-permute-start.27 = (bf16[1,32,1,1,8]{1,4,3,2,0:T(8,128)(2,1)S(1)}, bf16[1,32,1,1,8]{1,4,3,2,0:T(8,128)(2,1)S(1)}, u32[]{:S(2)}, u32[]{:S(2)}) collective-permute-start(bf16[1,32,1,1,8]{1,4,3,2,0:T(8,128)(2,1)S(1)} %get-tuple-element.1025), channel_id=1, source_target_pairs={{0,40},{1,41},{2,42},{3,43},{4,44},{5,45},{6,46},{7,47},{8,48},{9,... | collective-permute-start | bytes 1544 | tf_op jit(solution)/shard_map/ppermute | solution.py:17
  368.6 19.8 %collective-permute-start.28 = (bf16[1,32,1,1,1]{1,4,3,2,0:T(2,128)(2,1)S(1)}, bf16[1,32,1,1,1]{1,4,3,2,0:T(2,128)(2,1)S(1)}, u32[]{:S(2)}, u32[]{:S(2)}) collective-permute-start(bf16[1,32,1,1,1]{1,4,3,2,0:T(2,128)(2,1)S(1)} %get-tuple-element.1020), channel_id=1, source_target_pairs={{0,39},{1,40},{2,41},{3,42},{4,43},{5,44},{6,45},{7,46},{8,47},{9,... | collective-permute-start | bytes 200 | tf_op jit(solution)/shard_map/ppermute | solution.py:17
  369.3 85.4 %collective-permute-start.29 = (bf16[1,32,1,16,1]{1,4,3,2,0:T(2,128)(2,1)S(1)}, bf16[1,32,1,16,1]{1,4,3,2,0:T(2,128)(2,1)S(1)}, u32[]{:S(2)}, u32[]{:S(2)}) collective-permute-start(bf16[1,32,1,16,1]{1,4,3,2,0:T(2,128)(2,1)S(1)} %get-tuple-element.1029), channel_id=1, source_target_pairs={{0,33},{1,34},{2,35},{3,36},{4,37},{5,38},{6,39},{7,40},{8,41},{9,... | collective-permute-start | bytes 3080 | tf_op jit(solution)/shard_map/ppermute | solution.py:17
  370.0 131.2 %collective-permute-start.30 = (bf16[1,32,1,16,8]{1,4,3,2,0:T(8,128)(2,1)S(1)}, bf16[1,32,1,16,8]{1,4,3,2,0:T(8,128)(2,1)S(1)}, u32[]{:S(2)}, u32[]{:S(2)}) collective-permute-start(bf16[1,32,1,16,8]{1,4,3,2,0:T(8,128)(2,1)S(1)} %get-tuple-element.1031), channel_id=1, source_target_pairs={{0,32},{1,33},{2,34},{3,35},{4,36},{5,37},{6,38},{7,39},{8,40},{9,... | collective-permute-start | bytes 24584 | tf_op jit(solution)/shard_map/ppermute | solution.py:17
  383.0 78.5 %collective-permute-start.31 = (bf16[1,32,1,16,1]{1,4,3,2,0:T(2,128)(2,1)S(1)}, bf16[1,32,1,16,1]{1,4,3,2,0:T(2,128)(2,1)S(1)}, u32[]{:S(2)}, u32[]{:S(2)}) collective-permute-start(bf16[1,32,1,16,1]{1,4,3,2,0:T(2,128)(2,1)S(1)} %get-tuple-element.1028), channel_id=1, source_target_pairs={{0,31},{1,32},{2,33},{3,34},{4,35},{5,36},{6,37},{7,38},{8,39},{9,... | collective-permute-start | bytes 3080 | tf_op jit(solution)/shard_map/ppermute | solution.py:17
  422.6 18.6 %collective-permute-start.33 = (bf16[1,32,1,1,8]{1,4,3,2,0:T(8,128)(2,1)S(1)}, bf16[1,32,1,1,8]{1,4,3,2,0:T(8,128)(2,1)S(1)}, u32[]{:S(2)}, u32[]{:S(2)}) collective-permute-start(bf16[1,32,1,1,8]{1,4,3,2,0:T(8,128)(2,1)S(1)} %get-tuple-element.1024), channel_id=1, source_target_pairs={{0,24},{1,25},{2,26},{3,27},{4,28},{5,29},{6,30},{7,31},{8,32},{9,... | collective-permute-start | bytes 1544 | tf_op jit(solution)/shard_map/ppermute | solution.py:17
  438.7 24.8 %collective-permute-start.35 = (bf16[1,32,16,1,1]{1,4,3,2,0:T(2,128)(2,1)S(1)}, bf16[1,32,16,1,1]{1,4,3,2,0:T(2,128)(2,1)S(1)}, u32[]{:S(2)}, u32[]{:S(2)}) collective-permute-start(bf16[1,32,16,1,1]{1,4,3,2,0:T(2,128)(2,1)S(1)} %get-tuple-element.1035), channel_id=1, source_target_pairs={{0,9},{1,10},{2,11},{3,12},{4,13},{5,14},{6,15},{7,16},{8,17},{9,1... | collective-permute-start | bytes 3080 | tf_op jit(solution)/shard_map/ppermute | solution.py:17
  448.3 54.1 %collective-permute-start.36 = (bf16[1,32,16,1,8]{1,4,3,2,0:T(8,128)(2,1)S(1)}, bf16[1,32,16,1,8]{1,4,3,2,0:T(8,128)(2,1)S(1)}, u32[]{:S(2)}, u32[]{:S(2)}) collective-permute-start(bf16[1,32,16,1,8]{1,4,3,2,0:T(8,128)(2,1)S(1)} %get-tuple-element.1037), channel_id=1, source_target_pairs={{0,8},{1,9},{2,10},{3,11},{4,12},{5,13},{6,14},{7,15},{8,16},{9,17... | collective-permute-start | bytes 24584 | tf_op jit(solution)/shard_map/ppermute | solution.py:17
  461.5 42.5 %collective-permute-start.38 = (bf16[1,32,16,16,1]{1,4,3,2,0:T(2,128)(2,1)S(1)}, bf16[1,32,16,16,1]{1,4,3,2,0:T(2,128)(2,1)S(1)}, u32[]{:S(2)}, u32[]{:S(2)}) collective-permute-start(bf16[1,32,16,16,1]{1,4,3,2,0:T(2,128)(2,1)S(1)} %get-tuple-element.1039), channel_id=1, source_target_pairs={{0,1},{1,2},{2,3},{3,4},{4,5},{5,6},{6,7},{7,8},{8,9},{9,10},{10,1... | collective-permute-start | bytes 49160 | tf_op jit(solution)/shard_map/ppermute | solution.py:17
  463.5 43.5 %collective-permute-start.39 = (bf16[1,32,16,16,1]{1,4,3,2,0:T(2,128)(2,1)S(1)}, bf16[1,32,16,16,1]{1,4,3,2,0:T(2,128)(2,1)S(1)}, u32[]{:S(2)}, u32[]{:S(2)}) collective-permute-start(bf16[1,32,16,16,1]{1,4,3,2,0:T(2,128)(2,1)S(1)} %get-tuple-element.1038), channel_id=1, source_target_pairs={{1,0},{2,1},{3,2},{4,3},{5,4},{6,5},{7,6},{8,7},{9,8},{10,9},{11,1... | collective-permute-start | bytes 49160 | tf_op jit(solution)/shard_map/ppermute | solution.py:17
  542.4 19.6 %collective-permute-start.55 = (bf16[1,64,1,16,1]{1,0,4,3,2:T(2,128)(2,1)S(1)}, bf16[1,64,1,16,1]{1,0,4,3,2:T(2,128)(2,1)S(1)}, u32[]{:S(2)}, u32[]{:S(2)}) collective-permute-start(bf16[1,64,1,16,1]{1,0,4,3,2:T(2,128)(2,1)S(1)} %get-tuple-element.977), channel_id=1, source_target_pairs={{0,33},{1,34},{2,35},{3,36},{4,37},{5,38},{6,39},{7,40},{8,41},{9,... | collective-permute-start | bytes 6152 | tf_op jit(solution)/shard_map/ppermute | solution.py:17
  543.1 22.9 %collective-permute-start.56 = (bf16[1,64,1,16,8]{1,0,4,3,2:T(2,128)(2,1)S(1)}, bf16[1,64,1,16,8]{1,0,4,3,2:T(2,128)(2,1)S(1)}, u32[]{:S(2)}, u32[]{:S(2)}) collective-permute-start(bf16[1,64,1,16,8]{1,0,4,3,2:T(2,128)(2,1)S(1)} %get-tuple-element.979), channel_id=1, source_target_pairs={{0,32},{1,33},{2,34},{3,35},{4,36},{5,37},{6,38},{7,39},{8,40},{9,... | collective-permute-start | bytes 49160 | tf_op jit(solution)/shard_map/ppermute | solution.py:17
  546.0 22.6 %collective-permute-start.57 = (bf16[1,64,1,16,1]{1,0,4,3,2:T(2,128)(2,1)S(1)}, bf16[1,64,1,16,1]{1,0,4,3,2:T(2,128)(2,1)S(1)}, u32[]{:S(2)}, u32[]{:S(2)}) collective-permute-start(bf16[1,64,1,16,1]{1,0,4,3,2:T(2,128)(2,1)S(1)} %get-tuple-element.976), channel_id=1, source_target_pairs={{0,31},{1,32},{2,33},{3,34},{4,35},{5,36},{6,37},{7,38},{8,39},{9,... | collective-permute-start | bytes 6152 | tf_op jit(solution)/shard_map/ppermute | solution.py:17
  565.9 19.7 %collective-permute-start.61 = (bf16[1,64,16,1,1]{1,0,4,3,2:T(2,128)(2,1)S(1)}, bf16[1,64,16,1,1]{1,0,4,3,2:T(2,128)(2,1)S(1)}, u32[]{:S(2)}, u32[]{:S(2)}) collective-permute-start(bf16[1,64,16,1,1]{1,0,4,3,2:T(2,128)(2,1)S(1)} %get-tuple-element.983), channel_id=1, source_target_pairs={{0,9},{1,10},{2,11},{3,12},{4,13},{5,14},{6,15},{7,16},{8,17},{9,1... | collective-permute-start | bytes 6152 | tf_op jit(solution)/shard_map/ppermute | solution.py:17
  568.6 20.1 %collective-permute-start.62 = (bf16[1,64,16,1,8]{1,0,4,3,2:T(2,128)(2,1)S(1)}, bf16[1,64,16,1,8]{1,0,4,3,2:T(2,128)(2,1)S(1)}, u32[]{:S(2)}, u32[]{:S(2)}) collective-permute-start(bf16[1,64,16,1,8]{1,0,4,3,2:T(2,128)(2,1)S(1)} %get-tuple-element.985), channel_id=1, source_target_pairs={{0,8},{1,9},{2,10},{3,11},{4,12},{5,13},{6,14},{7,15},{8,16},{9,17... | collective-permute-start | bytes 49160 | tf_op jit(solution)/shard_map/ppermute | solution.py:17
  571.1 22.9 %collective-permute-start.63 = (bf16[1,64,16,1,1]{1,0,4,3,2:T(2,128)(2,1)S(1)}, bf16[1,64,16,1,1]{1,0,4,3,2:T(2,128)(2,1)S(1)}, u32[]{:S(2)}, u32[]{:S(2)}) collective-permute-start(bf16[1,64,16,1,1]{1,0,4,3,2:T(2,128)(2,1)S(1)} %get-tuple-element.982), channel_id=1, source_target_pairs={{0,7},{1,8},{2,9},{3,10},{4,11},{5,12},{6,13},{7,14},{8,15},{9,16}... | collective-permute-start | bytes 6152 | tf_op jit(solution)/shard_map/ppermute | solution.py:17
  575.6 29.8 %collective-permute-start.64 = (bf16[1,64,16,16,1]{1,0,4,3,2:T(2,128)(2,1)S(1)}, bf16[1,64,16,16,1]{1,0,4,3,2:T(2,128)(2,1)S(1)}, u32[]{:S(2)}, u32[]{:S(2)}) collective-permute-start(bf16[1,64,16,16,1]{1,0,4,3,2:T(2,128)(2,1)S(1)} %get-tuple-element.987), channel_id=1, source_target_pairs={{0,1},{1,2},{2,3},{3,4},{4,5},{5,6},{6,7},{7,8},{8,9},{9,10},{10,1... | collective-permute-start | bytes 98312 | tf_op jit(solution)/shard_map/ppermute | solution.py:17
  578.1 30.1 %collective-permute-start.65 = (bf16[1,64,16,16,1]{1,0,4,3,2:T(2,128)(2,1)S(1)}, bf16[1,64,16,16,1]{1,0,4,3,2:T(2,128)(2,1)S(1)}, u32[]{:S(2)}, u32[]{:S(2)}) collective-permute-start(bf16[1,64,16,16,1]{1,0,4,3,2:T(2,128)(2,1)S(1)} %get-tuple-element.986), channel_id=1, source_target_pairs={{1,0},{2,1},{3,2},{4,3},{5,4},{6,5},{7,6},{8,7},{9,8},{10,9},{11,1... | collective-permute-start | bytes 98312 | tf_op jit(solution)/shard_map/ppermute | solution.py:17
  585.6 25.3 %collective-permute-start.66 = (bf16[1,64,16,1,1]{1,0,4,3,2:T(2,128)(2,1)S(1)}, bf16[1,64,16,1,1]{1,0,4,3,2:T(2,128)(2,1)S(1)}, u32[]{:S(2)}, u32[]{:S(2)}) collective-permute-start(bf16[1,64,16,1,1]{1,0,4,3,2:T(2,128)(2,1)S(1)} %get-tuple-element.981), channel_id=1, source_target_pairs={{7,0},{8,1},{9,2},{10,3},{11,4},{12,5},{13,6},{14,7},{15,8},{16,9}... | collective-permute-start | bytes 6152 | tf_op jit(solution)/shard_map/ppermute | solution.py:17
  588.7 24.8 %collective-permute-start.67 = (bf16[1,64,16,1,8]{1,0,4,3,2:T(2,128)(2,1)S(1)}, bf16[1,64,16,1,8]{1,0,4,3,2:T(2,128)(2,1)S(1)}, u32[]{:S(2)}, u32[]{:S(2)}) collective-permute-start(bf16[1,64,16,1,8]{1,0,4,3,2:T(2,128)(2,1)S(1)} %get-tuple-element.984), channel_id=1, source_target_pairs={{8,0},{9,1},{10,2},{11,3},{12,4},{13,5},{14,6},{15,7},{16,8},{17,9... | collective-permute-start | bytes 49160 | tf_op jit(solution)/shard_map/ppermute | solution.py:17
  594.0 22.1 %collective-permute-start.68 = (bf16[1,64,16,1,1]{1,0,4,3,2:T(2,128)(2,1)S(1)}, bf16[1,64,16,1,1]{1,0,4,3,2:T(2,128)(2,1)S(1)}, u32[]{:S(2)}, u32[]{:S(2)}) collective-permute-start(bf16[1,64,16,1,1]{1,0,4,3,2:T(2,128)(2,1)S(1)} %get-tuple-element.980), channel_id=1, source_target_pairs={{9,0},{10,1},{11,2},{12,3},{13,4},{14,5},{15,6},{16,7},{17,8},{18,... | collective-permute-start | bytes 6152 | tf_op jit(solution)/shard_map/ppermute | solution.py:17
  (61 other events, 1498.3 us)
Sparse Core Ops, SparseCore 0:
  540.5 253.7 all-reduce.4
where the time goes:
time: 865 us; the launch traced here: 857 us
  starting transfers between devices  249 us (29%)
  local copies, waits for them, and re-layouts  215 us (25%)
  matrix products  177 us (20%)
  blocking collectives  80.5 us (9%)
  waiting for transfers between devices  75.9 us (9%)
  other arithmetic  43.7 us (5%)
  between operations  16.6 us (2%)
    ppermute x78, starting transfers between devices, passed_along(): return lax.ppermute(block, axis, route)  249 us
    scatter x55, local copies, waits for them, and re-layouts, extend(): grown = grown.at[:, :, high[0][0]:high[0][1], high[1][0]:high[1][1], high...  147 us
    transpose x2, matrix products, kernel_grad(): return result.transpose(1, 0, 2, 3, 4)  112 us
    psum x1, blocking collectives, on_device(): lax.psum((kernel_grad(padded_in, grad_first), kernel_grad(padded_mid, gra...  80.5 us
    ppermute x78, waiting for transfers between devices, passed_along(): return lax.ppermute(block, axis, route)  75.9 us
    conv_general_dilated x3, matrix products, convolve_valid(): lax.conv_general_dilated(padded, kernel, (1, 1, 1), 'VALID', dimension_nu...  64.6 us
    select_n x2, local copies, waits for them, and re-layouts, leaky(): return jnp.where(values > 0, values, SLOPE * values)  19.7 us
  transfers between devices with their start and end apart: 79, of which 22 were waited for; matrix products, arithmetic and copies ran while one was open for 27% of the time, Pallas kernels for 0%

commit v1 on v0

v1 whole, which is shorter than its diff:
```python
import functools

import jax
import jax.numpy as jnp
import numpy as np
from jax import lax
from jax.experimental import pallas as pl
from jax.experimental.pallas import tpu as pltpu
from jax.sharding import PartitionSpec as P

F32 = jnp.float32
BF16 = jnp.bfloat16
PY, PZ = 4, 8
NY = 4
KRAW = 1408
MESH = pl.DeviceIdType.MESH


def plane_order(rim):
    lanes = {(y, z): y * 8 + z for y in range(16) for z in range(8)}
    for y in range(-rim, 16 + rim):
        for z in range(-rim, 8 + rim):
            if (y, z) not in lanes:
                lanes[(y, z)] = len(lanes)
    return lanes


def raw_lane(y, z):
    row = y + 5 if y < 0 else y - 32
    col = z + 5 if z < 0 else z - 16
    if 0 <= y < 32 and 0 <= z < 16:
        return y * 16 + z
    if 0 <= z < 16:
        return (512 if y < 0 else 640) + row * 16 + z
    if 0 <= y < 32:
        return (768 if z < 0 else 1024) + col * 32 + y
    return 1280 + ((y >= 32) * 2 + (z >= 16)) * 32 + row * 5 + col


@functools.cache
def matrices():
    wide, ring = plane_order(2), plane_order(1)
    gather = np.zeros((16, KRAW, 256), np.float32)
    for dy in range(4):
        for dz in range(4):
            for (y, z), lane in wide.items():
                gather[dy * 4 + dz, raw_lane(2 * y - 1 + dy, 2 * z - 1 + dz), lane] = 1
    outgoing = np.zeros((512, 896), np.float32)
    for r in range(5):
        for z in range(16):
            outgoing[(27 + r) * 16 + z, r * 16 + z] = 1
            outgoing[r * 16 + z, 128 + r * 16 + z] = 1
    for c in range(5):
        for y in range(32):
            outgoing[y * 16 + 11 + c, 256 + c * 32 + y] = 1
            outgoing[y * 16 + c, 512 + c * 32 + y] = 1
    for k in range(4):
        for r in range(5):
            for c in range(5):
                y = r if k // 2 else 27 + r
                z = c if k % 2 else 11 + c
                outgoing[y * 16 + z, 768 + k * 32 + r * 5 + c] = 1
    second = np.zeros((9, 256, 256), np.float32)
    back = np.zeros((5, 256, 256), np.float32)
    for dy in range(3):
        for dz in range(3):
            tap = dy * 3 + dz
            for (y, z), lane in ring.items():
                second[tap, wide[(y + dy - 1, z + dz - 1)], lane] = 1
            for y in range(16):
                for z in range(8):
                    source = ring[(y - dy + 1, z - dz + 1)]
                    back[tap // 2, source, (tap % 2) * 128 + y * 8 + z] = 1
    fold = np.zeros((128, 2048), np.float32)
    for phase in range(8):
        px, py, pz = phase // 4, phase // 2 % 2, phase % 2
        for tx in range(3):
            for ty in range(3):
                for tz in range(3):
                    for channel in range(4):
                        x, y, z = tx + px, ty + py, tz + pz
                        row = (y * 4 + z) * 16 + ((x - 1) % 4) * 4 + channel
                        fold[((tx * 3 + ty) * 3 + tz) * 4 + channel, phase * 256 + row] = 1
    pool = np.zeros((512, 128), np.float32)
    for x in range(4):
        for y in range(16):
            for z in range(8):
                pool[x * 128 + y * 8 + z, x * 32 + (y // 2) * 4 + z // 2] = 1
    cot_out = np.zeros((256, 256), np.float32)
    cot_in = np.zeros((384, 1024), np.float32)
    for x in range(8):
        for y in range(8):
            cot_out[x * 32 + y * 4, x * 8 + y] = 1
            cot_out[x * 32 + y * 4 + 3, 64 + x * 8 + y] = 1
        for z in range(4):
            cot_out[x * 32 + z, 128 + x * 4 + z] = 1
            cot_out[x * 32 + 28 + z, 160 + x * 4 + z] = 1
        for (y, z), lane in ring.items():
            if lane < 128:
                continue
            if 0 <= y < 16:
                source = x * 8 + y // 2 + (64 if z < 0 else 0)
            elif 0 <= z < 8:
                source = 128 + x * 4 + z // 2 + (32 if y < 0 else 0)
            else:
                source = 256 + x * 4 + (3 if z < 0 else 0) + (32 if y < 0 else 0)
            cot_in[source, x * 128 + lane - 128] = 1
    sides = np.zeros((8, 256), np.float32)
    for (y, z), lane in wide.items():
        sides[:4, lane] = (y < 0, y >= 16, z < 0, z >= 8)
    sixteen = (gather, outgoing, second, back, fold, pool, cot_out, cot_in)
    return tuple(m.astype(jnp.bfloat16) for m in sixteen) + (sides,)


def mm(a, b):
    return jnp.dot(a, b, preferred_element_type=F32)


def mm_nt(a, b):
    return lax.dot_general(a, b, (((1,), (1,)), ((), ())), preferred_element_type=F32)


def identity(n):
    rows = lax.broadcasted_iota(jnp.int32, (n, n), 0)
    return jnp.where(rows == lax.broadcasted_iota(jnp.int32, (n, n), 1), 1.0, 0.0).astype(BF16)


def leaky(t):
    return jnp.where(t > 0, t, 0.3 * t)


def slope(t):
    return jnp.where(t > 0, jnp.float32(1.0), jnp.float32(0.3))


def split(t):
    high = t.astype(BF16)
    return high, (t - high.astype(F32)).astype(BF16)


FACES = ((1, 0), (-1, 0), (0, 1), (0, -1))
CORNERS = ((1, 1), (1, -1), (-1, 1), (-1, -1))
DIRS = FACES + CORNERS
XY = tuple((a, b) for a in range(4) for b in range(4) if (a, b) != (0, 0))
S_RAW, S_COT, S_CORE, S_XY, S_Z, S_AG = 0, 8, 16, 24, 40, 48


def body(
    vol, k1, w2, cot, gather_h, outgoing_h, second_h, back_h, fold_h, pool_h, cot_out_h, cot_in_h, sides,
    feat_out, grad_out, first_out, second_out,
    gather, outgoing, second, back, fold, pool, cot_out, cot_in,
    rows32, lraw, sy_buf, sz_buf, sc_buf, ry_buf, rz_buf, rc_buf, edge_in,
    cot_send, cot_recv, x4, x4i, pre1, weights1, forward2, backward2, k1s,
    p2, b2i, b2r, t2i, t2r, spread_i, spread_r, pooled, pg, gshift, bg, t3, g1,
    total, core_in, xy_in, z_in, final,
    local_sem, send_sem, recv_sem,
):
    dp, g, s = lax.axis_index("dp"), lax.axis_index("gx"), lax.axis_index("yz")
    by, bz = s // PZ, s % PZ
    yi, zi = s % NY, s // NY
    other = (dp, 1 - g, s)
    near = [(dp, g, ((by + a) % PY) * PZ + (bz + b) % PZ) for a, b in DIRS]
    flat = [((dp + a) % 4, g, zi * NY + (yi + b) % NY) for a, b in XY]
    tall = [(dp, g, ((zi + k) % 8) * NY + yi) for k in range(1, 8)]

    loads = [
        pltpu.make_async_copy(a, b, local_sem.at[i])
        for i, (a, b) in enumerate(
            (
                (outgoing_h, outgoing), (cot_out_h, cot_out), (fold_h, fold), (pool_h, pool), (cot_in_h, cot_in),
                (gather_h, gather), (second_h, second), (back_h, back),
            )
        )
    ]
    for load in loads:
        load.start()

    barrier = pltpu.get_barrier_semaphore()
    everyone = [other] + near + flat + tall
    for device in everyone:
        pl.semaphore_signal(barrier, inc=1, device_id=device, device_id_type=MESH)

    def remote(source, target, slot, device):
        return pltpu.make_async_remote_copy(
            src_ref=source, dst_ref=target, send_sem=send_sem.at[slot], recv_sem=recv_sem.at[slot],
            device_id=device, device_id_type=MESH,
        )

    def valid(a, b):
        ok = jnp.logical_and(
            jnp.logical_and(by + a >= 0, by + a < PY), jnp.logical_and(bz + b >= 0, bz + b < PZ)
        )
        return jnp.where(ok, jnp.float32(1.0), jnp.float32(0.0))

    lane = lax.broadcasted_iota(jnp.int32, (1, 128), 1)

    for x in range(32):
        rows32[4 * x : 4 * x + 4, :] = vol[:, x * 512 : (x + 1) * 512].astype(F32)
    lraw[0:128, 0:512] = rows32[...].astype(BF16)
    loads[0].wait()
    out = mm(lraw[0:128, 0:512], outgoing[...])
    sy_buf[0] = (out[:, 0:128] * valid(1, 0)).astype(BF16)
    sy_buf[1] = (out[:, 128:256] * valid(-1, 0)).astype(BF16)
    sz_buf[0] = (out[:, 256:512] * valid(0, 1)).astype(BF16)
    sz_buf[1] = (out[:, 512:768] * valid(0, -1)).astype(BF16)
    for k, (a, b) in enumerate(CORNERS):
        packed = jnp.zeros((32, 128), F32)
        for j in range(4):
            piece = out[32 * j : 32 * j + 32, 768:896]
            moved = pltpu.roll(piece, (32 * (j - k)) % 128, 1) if j != k else piece
            packed = jnp.where(lane // 32 == j, moved, packed)
        sc_buf[k] = (packed * valid(a, b)).astype(BF16)
    loads[1].wait()
    strips = mm(cot[...], cot_out[...])
    for i, (a, b) in enumerate(DIRS):
        part = strips[:, 0:128] if a == 0 else strips[:, 128:256]
        cot_send[i] = (part * valid(a, b)).astype(BF16)

    pl.semaphore_wait(barrier, len(everyone))
    raw_copies = []
    for i in (4, 5, 6, 7, 0, 1, 2, 3):
        if i >= 4:
            pair = (sc_buf.at[i - 4], rc_buf.at[i - 4])
        elif i >= 2:
            pair = (sz_buf.at[i - 2], rz_buf.at[i - 2])
        else:
            pair = (sy_buf.at[i], ry_buf.at[i])
        copy = remote(pair[0], pair[1], S_RAW + i, near[i])
        copy.start()
        raw_copies.append(copy)
    cot_copies = []
    for i in range(8):
        copy = remote(cot_send.at[i], cot_recv.at[i], S_COT + i, near[i])
        copy.start()
        cot_copies.append(copy)

    k1s[...] = jnp.zeros_like(k1s)
    for tap in range(27):
        k1s[4 * tap : 4 * tap + 4, :] = k1[tap].astype(F32)
    loads[2].wait()
    k1t = mm_nt(identity(32), k1s[...].astype(BF16)).astype(BF16)
    for phase in range(8):
        weights1[32 * phase : 32 * phase + 32, :] = mm(k1t, fold[:, 256 * phase : 256 * phase + 256]).astype(BF16)
    eye = identity(64)
    for x in range(3):
        block = w2[9 * x : 9 * x + 9].reshape(288, 64)
        forward2[64 * x : 64 * x + 64, :] = mm_nt(eye, block).astype(BF16)
        for a in (0, 2, 4, 6):
            both = jnp.concatenate([w2[9 * x + a].astype(F32), w2[9 * x + a + 1].astype(F32)], axis=1)
            backward2[32 * x : 32 * x + 32, 64 * a : 64 * a + 128] = both.astype(BF16)
        backward2[32 * x : 32 * x + 32, 512:576] = w2[9 * x + 8]
    loads[3].wait()
    for half in range(2):
        spread_i[:, 512 * half : 512 * half + 512] = mm_nt(cot[:, 128 * half : 128 * half + 128], pool[...])
    far = pl.multiple_of(g * (17 * 32), 32)
    p2[pl.ds(far, 32), :] = jnp.zeros((32, 256), BF16)
    far = pl.multiple_of(g * (17 * 64), 64)
    pg[pl.ds(far, 64), :] = jnp.zeros((64, 256), BF16)
    gshift[...] = jnp.zeros_like(gshift)
    lraw[128:144, :] = jnp.zeros((16, KRAW), BF16)
    for load in loads[4:]:
        load.wait()

    for copy in raw_copies:
        copy.wait_recv()
    lraw[0:128, 512:640] = ry_buf[0]
    lraw[0:128, 640:768] = ry_buf[1]
    lraw[0:128, 768:1024] = rz_buf[0]
    lraw[0:128, 1024:1280] = rz_buf[1]
    for j in range(4):
        corner = jnp.zeros((32, 128), F32)
        for k in range(4):
            piece = rc_buf[k].astype(F32)
            moved = pltpu.roll(piece, (32 * (k - j)) % 128, 1) if j != k else piece
            corner = jnp.where(lane // 32 == k, moved, corner)
        lraw[32 * j : 32 * j + 32, 1280:1408] = corner.astype(BF16)
    mine = pl.multiple_of(jnp.where(g == 0, 112, 0), 16)
    copy = remote(lraw.at[pl.ds(mine, 16), :], edge_in, S_CORE, other)
    copy.start()
    core_copies = [copy]
    copy.wait_recv()
    first_core = jnp.where(g == 0, jnp.float32(1.0), jnp.float32(0.0))
    edge = edge_in[...].astype(F32)
    half_row = lax.broadcasted_iota(jnp.int32, (8, 1), 0)
    edge = jnp.where(half_row < 4, edge[0:8] * first_core, edge[8:16] * (1.0 - first_core))
    lraw[128:144, :] = jnp.concatenate([edge, jnp.zeros_like(edge)], axis=0).astype(BF16)

    def gather_step(tap, carry):
        got = mm(lraw[...], gather[tap])
        low = half_row < 4
        at = pl.multiple_of(tap * 16, 16)
        for x in range(16):
            after = got[8 * x + 8 : 8 * x + 16]
            before = got[8 * x - 8 : 8 * x] if x else got[128:136]
            block = jnp.concatenate([got[8 * x : 8 * x + 8], jnp.where(low, after, before)], axis=0).astype(BF16)
            x4[x, pl.ds(at, 16), :] = block
            x4i[pl.ds(at, 16), 128 * x : 128 * x + 128] = block[:, 0:128]
        return carry

    lax.fori_loop(0, 16, gather_step, 0)

    def flag(test):
        return jnp.where(test, jnp.float32(1.0), jnp.float32(0.0))

    outside = jnp.maximum(
        jnp.maximum(sides[0:1, :] * flag(by == 0), sides[1:2, :] * flag(by == PY - 1)),
        jnp.maximum(sides[2:3, :] * flag(bz == 0), sides[3:4, :] * flag(bz == PZ - 1)),
    )
    scale = (1.0 - outside) * 0.125

    def first_layer(x, carry):
        pre = mm(weights1[...], x4[x])
        pre1[x] = pre[:, 0:128]
        act = leaky(pre[0:32])
        for phase in range(1, 8):
            act = act + leaky(pre[32 * phase : 32 * phase + 32])
        p2[pl.ds(pl.multiple_of(32 * x + 32, 32), 32), :] = (act * scale).astype(BF16)
        return carry

    lax.fori_loop(0, 16, first_layer, 0)
    near_src = pl.multiple_of(jnp.where(g == 0, 16 * 32, 32), 32)
    near_dst = pl.multiple_of(jnp.where(g == 0, 0, 17 * 32), 32)
    copy = remote(p2.at[pl.ds(near_src, 32), :], p2.at[pl.ds(near_dst, 32), :], S_CORE + 1, other)
    copy.start()
    core_copies.append(copy)

    for cot_copy in cot_copies:
        cot_copy.wait_recv()
    down, up, left, right = (cot_recv[i] for i in range(4))
    zs = jnp.where(lane >= 64, left.astype(F32), right.astype(F32))
    ys = jnp.where(lane >= 32, down.astype(F32), up.astype(F32))
    late = lane % 4 == 3
    cs = jnp.where(
        lane >= 32,
        jnp.where(late, cot_recv[4].astype(F32), cot_recv[5].astype(F32)),
        jnp.where(late, cot_recv[6].astype(F32), cot_recv[7].astype(F32)),
    )
    rim = jnp.concatenate([zs, ys, cs], axis=1).astype(BF16)
    spread_r[...] = mm(rim, cot_in[...])

    copy.wait_recv()

    def shift_step(tap, carry):
        got = mm(p2[...], second[tap])
        at = pl.multiple_of(tap * 32, 32)
        for x in range(18):
            block = got[32 * x : 32 * x + 32].astype(BF16)
            b2i[pl.ds(at, 32), 128 * x : 128 * x + 128] = block[:, 0:128]
            b2r[pl.ds(at, 32), 128 * x : 128 * x + 128] = block[:, 128:256]
        return carry

    lax.fori_loop(0, 9, shift_step, 0)

    def second_layer(chunk, carry):
        at = pl.ds(pl.multiple_of(chunk * 256, 256), 256)
        t2i[:, at] = mm(forward2[...], b2i[:, at])
        t2r[:, at] = mm(forward2[...], b2r[:, at])
        return carry

    lax.fori_loop(0, 9, second_layer, 0)

    for half in range(8):
        lifted = spread_i[:, 128 * half : 128 * half + 128] * 0.125
        lifted_rim = spread_r[:, 128 * half : 128 * half + 128] * 0.125
        pair = jnp.zeros((64, 128), F32)
        for x in (2 * half, 2 * half + 1):
            at = [slice(128 * (x + d), 128 * (x + d) + 128) for d in range(3)]
            pre = t2i[0:64, at[0]] + t2i[64:128, at[1]] + t2i[128:192, at[2]]
            pair = pair + leaky(pre)
            grad = (lifted * slope(pre)).astype(BF16)
            pg[64 * x + 64 : 64 * x + 128, 0:128] = grad
            for d in range(3):
                gshift[64 * d : 64 * d + 64, at[d]] = grad
            pre = t2r[0:64, at[0]] + t2r[64:128, at[1]] + t2r[128:192, at[2]]
            pg[64 * x + 64 : 64 * x + 128, 128:256] = (lifted_rim * slope(pre)).astype(BF16)
        high, low = split(pair)
        at = slice(128 * (half % 4), 128 * (half % 4) + 128)
        pooled[half // 4, 0:64, at] = high
        pooled[half // 4, 64:128, at] = low
    near_src = pl.multiple_of(jnp.where(g == 0, 16 * 64, 64), 64)
    near_dst = pl.multiple_of(jnp.where(g == 0, 0, 17 * 64), 64)
    copy = remote(pg.at[pl.ds(near_src, 64), :], pg.at[pl.ds(near_dst, 64), :], S_CORE + 2, other)
    copy.start()
    core_copies.append(copy)
    for half in range(2):
        sums = mm(pooled[half], pool[...])
        feat_out[:, 128 * half : 128 * half + 128] = ((sums[0:64] + sums[64:128]) * 0.125).astype(BF16)

    grad2 = mm_nt(b2i[...], gshift[...])
    total[0:288, :] = grad2[:, 0:128]
    total[288:432, 0:64] = grad2[0:144, 128:192]
    total[288:432, 64:128] = grad2[144:288, 128:192]
    total[464:512, :] = jnp.zeros((48, 128), F32)
    copy.wait_recv()

    def back_step(step, carry):
        got = mm(pg[...], back[step])
        at = pl.multiple_of(step * 128, 128)
        for x in range(18):
            block = got[64 * x : 64 * x + 64].astype(BF16)
            bg[pl.ds(at, 64), 128 * x : 128 * x + 128] = block[:, 0:128]
            bg[pl.ds(at + 64, 64), 128 * x : 128 * x + 128] = block[:, 128:256]
        return carry

    lax.fori_loop(0, 5, back_step, 0)

    def back_layer(chunk, carry):
        at = pl.ds(pl.multiple_of(chunk * 256, 256), 256)
        t3[:, at] = mm(backward2[...], bg[0:576, at])
        return carry

    lax.fori_loop(0, 9, back_layer, 0)

    for x in range(16):
        grad = (
            t3[0:32, 128 * (x + 2) : 128 * (x + 3)]
            + t3[32:64, 128 * (x + 1) : 128 * (x + 2)]
            + t3[64:96, 128 * x : 128 * (x + 1)]
        )
        grad_out[pl.ds(x, 32, stride=16), :] = grad
        eighth = grad * 0.125
        for phase in range(8):
            at = slice(32 * phase, 32 * phase + 32)
            g1[at, 128 * x : 128 * x + 128] = (eighth * slope(pre1[x, at, :])).astype(BF16)
    wide = mm_nt(g1[...], x4i[...])
    partial = jnp.zeros((64, 128), F32)
    for phase in range(8):
        high, low = split(wide[32 * phase : 32 * phase + 32])
        partial = partial + mm_nt(jnp.concatenate([high, low], axis=0), fold[:, 256 * phase : 256 * phase + 256])
    total[432:464, :] = partial[0:32] + partial[32:64]

    mine = pl.multiple_of(g * 256, 256)
    theirs = pl.multiple_of((1 - g) * 256, 256)
    copy = remote(total.at[pl.ds(theirs, 256), :], core_in, S_CORE + 3, other)
    copy.start()
    copy.wait()
    core_in[...] = core_in[...] + total[pl.ds(mine, 256), :]
    xy_copies = []
    for i, (a, b) in enumerate(XY):
        piece = ((dp + a) % 4) * 4 + (yi + b) % 4
        source = core_in.at[pl.ds(pl.multiple_of(piece * 16, 16), 16), :]
        copy = remote(source, xy_in.at[i], S_XY + i, flat[i])
        copy.start()
        xy_copies.append(copy)
    place = pl.multiple_of((dp * 4 + yi) * 16, 16)
    part = core_in[pl.ds(place, 16), :]
    for i, copy in enumerate(xy_copies):
        copy.wait_recv()
        part = part + xy_in[i]
    z_in[zi] = part
    z_copies = []
    for k in range(7):
        copy = remote(z_in.at[zi], z_in.at[zi], S_Z + k, tall[k])
        copy.start()
        z_copies.append(copy)
    for copy in z_copies:
        copy.wait_recv()
    part = z_in[0]
    for k in range(1, 8):
        part = part + z_in[k]
    rows = pl.ds(pl.multiple_of(mine + place, 16), 16)
    final[rows, :] = part
    ag_copies = []
    for i in range(15):
        copy = remote(final.at[rows, :], final.at[rows, :], S_AG + i, flat[i])
        copy.start()
        ag_copies.append(copy)
    for copy in ag_copies:
        copy.wait_recv()
    half = pl.ds(mine, 256)
    copy = remote(final.at[half, :], final.at[half, :], S_CORE + 4, other)
    copy.start()
    core_copies.append(copy)
    copy.wait_recv()

    for a in range(9):
        at = slice(32 * a, 32 * a + 32)
        second_out[a] = final[at, 0:64]
        second_out[9 + a] = final[at, 64:128]
    for a in range(36):
        row = 288 + (8 * a) % 144
        lanes = slice(0, 64) if a < 18 else slice(64, 128)
        second_out[18 + a // 4, 8 * (a % 4) : 8 * (a % 4) + 8, :] = final[row : row + 8, lanes]
    flipped = final[432:464, :].T
    for tap in range(27):
        first_out[tap] = flipped[4 * tap : 4 * tap + 4, :]

    for copy in raw_copies + cot_copies + core_copies + xy_copies + z_copies + ag_copies:
        copy.wait_send()


def on_device(volumes, first_kernel, second_kernel, cotangent):
    consts = matrices()
    here = pl.BlockSpec(memory_space=pltpu.VMEM)
    there = pl.BlockSpec(memory_space=pl.ANY)
    vmem = pltpu.VMEM
    scratch = [vmem(m.shape, BF16) for m in consts[:8]] + [
        vmem((128, 512), F32), vmem((144, KRAW), BF16),
        vmem((2, 128, 128), BF16), vmem((2, 128, 256), BF16), vmem((4, 32, 128), BF16),
        vmem((2, 128, 128), BF16), vmem((2, 128, 256), BF16), vmem((4, 32, 128), BF16), vmem((16, KRAW), BF16),
        vmem((8, 64, 128), BF16), vmem((8, 64, 128), BF16),
        vmem((16, 256, 256), BF16), vmem((256, 2048), BF16), vmem((16, 256, 128), F32),
        vmem((256, 256), BF16), vmem((192, 288), BF16), vmem((96, 576), BF16), vmem((128, 32), F32),
        vmem((576, 256), BF16), vmem((288, 2304), BF16), vmem((288, 2304), BF16),
        vmem((192, 2304), F32), vmem((192, 2304), F32), vmem((64, 1024), F32), vmem((64, 1024), F32),
        vmem((2, 128, 512), BF16), vmem((1152, 256), BF16), vmem((192, 2304), BF16),
        vmem((640, 2304), BF16), vmem((96, 2304), F32), vmem((256, 2048), BF16),
        vmem((512, 128), F32), vmem((256, 128), F32), vmem((15, 16, 128), F32), vmem((8, 16, 128), F32), vmem((512, 128), F32),
        pltpu.SemaphoreType.DMA((8,)), pltpu.SemaphoreType.DMA((63,)), pltpu.SemaphoreType.DMA((63,)),
    ]
    features, act_grad, first_grad, second_grad = pl.pallas_call(
        body,
        out_shape=(
            jax.ShapeDtypeStruct((64, 256), BF16),
            jax.ShapeDtypeStruct((512, 128), F32),
            jax.ShapeDtypeStruct((27, 4, 32), F32),
            jax.ShapeDtypeStruct((27, 32, 64), F32),
        ),
        in_specs=[here] * 4 + [there] * 8 + [here],
        out_specs=(here,) * 4,
        scratch_shapes=scratch,
        compiler_params=pltpu.CompilerParams(
            collective_id=0, has_side_effects=True, vmem_limit_bytes=56 * 1024 * 1024
        ),
    )(
        volumes.reshape(4, 16384),
        first_kernel.transpose(2, 3, 4, 1, 0).reshape(27, 4, 32),
        second_kernel.transpose(2, 3, 4, 1, 0).reshape(27, 32, 64),
        cotangent.reshape(64, 256),
        *(jnp.asarray(m) for m in consts),
    )
    return (
        features.reshape(1, 64, 1, 1, 256),
        act_grad.reshape(1, 32, 1, 1, 2048),
        first_grad.reshape(3, 3, 3, 4, 32).transpose(4, 3, 0, 1, 2),
        second_grad.reshape(3, 3, 3, 32, 64).transpose(4, 3, 0, 1, 2),
    )


def solution(mesh):
    placed = (P("dp", None, "gx", "yz", None), P(), P(), P("dp", None, "gx", "yz", None))
    return jax.shard_map(
        on_device,
        mesh=mesh,
        in_specs=placed,
        out_specs=(P("dp", None, "gx", "yz", None), P("dp", None, "gx", "yz", None), P(), P()),
        check_vma=False,
    )
```

time: 865 us -> 67.1 us (0.08)
  starting transfers between devices: 249 us -> 0 us
  local copies, waits for them, and re-layouts: 215 us -> 6.29 us
  matrix products: 177 us -> 0 us
  blocking collectives: 80.5 us -> 0 us
  waiting for transfers between devices: 75.9 us -> 0 us
  Pallas kernels: 0 us -> 59.9 us
  other arithmetic: 43.7 us -> 0 us
  between operations: 16.6 us -> 0.64 us
    ppermute x78 -> x0, starting transfers between devices: 249 us -> none  [passed_along(): return lax.ppermute(block, axis, route)]
    scatter x55 -> x0, local copies, waits for them, and re-layouts: 147 us -> none  [extend(): grown = grown.at[:, :, high[0][0]:high[0][1], high[1][0]:high[1][1], high...]
    transpose x2 -> x0, matrix products: 112 us -> none  [kernel_grad(): return result.transpose(1, 0, 2, 3, 4)]
    psum x1 -> x0, blocking collectives: 80.5 us -> none  [on_device(): lax.psum((kernel_grad(padded_in, grad_first), kernel_grad(padded_mid, gra...]
    ppermute x78 -> x0, waiting for transfers between devices: 75.9 us -> none  [passed_along(): return lax.ppermute(block, axis, route)]
    conv_general_dilated x3 -> x0, matrix products: 64.6 us -> none  [convolve_valid(): lax.conv_general_dilated(padded, kernel, (1, 1, 1), 'VALID', dimension_nu...]
    pallas_call x0 -> x1, Pallas kernels: none -> 59.9 us  [on_device(): pl.pallas_call(body, out_shape=(jax.ShapeDtypeStruct((64, 256), BF16), ja...]
    select_n x3 -> x0, local copies, waits for them, and re-layouts: 31.2 us -> none  [the longest x2 19.7 us: leaky(): return jnp.where(values > 0, values, SLOPE * values)]
  transfers between devices with their start and end apart: 79 -> 0, of which waited for: 22 -> 0; matrix products, arithmetic and copies ran while one was open for 27% -> 0% of each run, Pallas kernels for 0% -> 0%
where the time goes in v1:
time: 67.1 us; the launch traced here: 66.8 us
  Pallas kernels  59.9 us (89%)
  local copies, waits for them, and re-layouts  6.29 us (9%)
    pallas_call x1, Pallas kernels, on_device(): pl.pallas_call(body, out_shape=(jax.ShapeDtypeStruct((64, 256), BF16), ja...  59.9 us
    unnamed x4, local copies, waits for them, and re-layouts  6.29 us

profile of v1, /device:TPU:1, one launch (start us, length us, event | category | flops | bytes accessed | tf_op | source)
XLA Modules:
  0.0 66.8 jit_solution(17232227916564849013)
XLA Ops:
  0.6 59.9 %shard_map.156 = (bf16[64,256]{1,0:T(8,128)(2,1)}, f32[512,128]{1,0:T(8,128)}, f32[27,4,32]{2,1,0:T(4,128)}, f32[27,32,64]{2,1,0:T(8,128)}) custom-call(bf16[4,16384]{1,0:T(4,128)(2,1)} %bitcast.19, bf16[27,4,32]{2,1,0:T(4,128)(2,1)} %bitcast.23, bf16[27,32,64]{2,1,0:T(8,128)(2,1)} %bitcast.18, bf16[64,256]{1,0:T(8,128)(2,1)} %bitcast.21, ...), custom_call_target="tpu_custom_call" | custom-call | tf_op jit(solution)/shard_map/pallas_call | solution.py:511
  60.5 1.4 %copy.22 = bf16[1,64,1,1,256]{4,1,3,2,0:T(8,128)(2,1)} copy(bf16[1,64,1,1,256]{4,1,3,2,0:T(8,128)(2,1)} %bitcast.22) | data formatting | bytes 65536
  61.9 1.7 %copy.23 = f32[1,32,1,1,2048]{4,3,2,1,0:T(1,128)} copy(f32[1,32,1,1,2048]{4,3,2,1,0:T(1,128)} %bitcast.17) | data formatting | bytes 524288
  63.5 1.4 %copy.24 = f32[32,4,3,3,3]{0,1,4,3,2:T(4,128)} copy(f32[32,4,3,3,3]{0,1,4,3,2:T(4,128)} %bitcast.20) | data formatting | bytes 27648
  65.0 1.8 %copy.25 = f32[64,32,3,3,3]{0,1,4,3,2:T(8,128)} copy(f32[64,32,3,3,3]{0,1,4,3,2:T(8,128)} %bitcast.16) | data formatting | bytes 442368

commit v2 on v1

--- a/solution.py
+++ b/solution.py
@@ -12,7 +12,7 @@
 BF16 = jnp.bfloat16
 PY, PZ = 4, 8
 NY = 4
-KRAW = 1408
+KRAW = 1280
 MESH = pl.DeviceIdType.MESH
 
 
@@ -25,41 +25,68 @@
     return lanes
 
 
-def raw_lane(y, z):
+def on_edge(y, z):
+    return y in (0, 31) or z in (0, 15)
+
+
+EDGE = {place: i for i, place in enumerate((y, z) for y in range(32) for z in range(16) if on_edge(y, z))}
+
+
+def rim_lane(y, z):
+    if 0 <= y < 32 and 0 <= z < 16:
+        return 640 + EDGE[(y, z)]
+    if 0 <= z < 16:
+        if y in (-1, 32):
+            return (0 if y < 0 else 16) + z
+        return 256 + ((y + 5) * 16 if y < 0 else 64 + (y - 33) * 16) + z
+    if 0 <= y < 32:
+        if z in (-1, 16):
+            return (32 if z < 0 else 64) + y
+        return 384 + ((z + 5) * 32 if z < 0 else 128 + (z - 17) * 32) + y
     row = y + 5 if y < 0 else y - 32
     col = z + 5 if z < 0 else z - 16
-    if 0 <= y < 32 and 0 <= z < 16:
-        return y * 16 + z
-    if 0 <= z < 16:
-        return (512 if y < 0 else 640) + row * 16 + z
-    if 0 <= y < 32:
-        return (768 if z < 0 else 1024) + col * 32 + y
-    return 1280 + ((y >= 32) * 2 + (z >= 16)) * 32 + row * 5 + col
+    return 128 + ((y >= 32) * 2 + (z >= 16)) * 32 + row * 5 + col
 
 
 @functools.cache
 def matrices():
     wide, ring = plane_order(2), plane_order(1)
-    gather = np.zeros((16, KRAW, 256), np.float32)
+    inside = np.zeros((8, 512, 256), np.float32)
+    nearby = np.zeros((8, 256, 256), np.float32)
+    around = np.zeros((8, 768, 256), np.float32)
     for dy in range(4):
         for dz in range(4):
-            for (y, z), lane in wide.items():
-                gather[dy * 4 + dz, raw_lane(2 * y - 1 + dy, 2 * z - 1 + dz), lane] = 1
-    outgoing = np.zeros((512, 896), np.float32)
-    for r in range(5):
+            step, shift = divmod(dy * 4 + dz, 2)
+            for (qy, qz), lane in wide.items():
+                y, z = 2 * qy - 1 + dy, 2 * qz - 1 + dz
+                if lane >= 128:
+                    around[step, rim_lane(y, z), shift * 128 + lane - 128] = 1
+                elif 0 <= y < 32 and 0 <= z < 16:
+                    inside[step, y * 16 + z, shift * 128 + lane] = 1
+                else:
+                    nearby[step, rim_lane(y, z), shift * 128 + lane] = 1
+    outgoing = np.zeros((512, 768), np.float32)
+    for r in range(4):
         for z in range(16):
             outgoing[(27 + r) * 16 + z, r * 16 + z] = 1
-            outgoing[r * 16 + z, 128 + r * 16 + z] = 1
-    for c in range(5):
-        for y in range(32):
+            outgoing[(1 + r) * 16 + z, 64 + r * 16 + z] = 1
+    for z in range(16):
+        outgoing[31 * 16 + z, 128 + z] = 1
+        outgoing[z, 144 + z] = 1
+    for y in range(32):
+        outgoing[y * 16 + 15, 160 + y] = 1
+        outgoing[y * 16, 192 + y] = 1
+        for c in range(4):
             outgoing[y * 16 + 11 + c, 256 + c * 32 + y] = 1
-            outgoing[y * 16 + c, 512 + c * 32 + y] = 1
+            outgoing[y * 16 + 1 + c, 384 + c * 32 + y] = 1
     for k in range(4):
         for r in range(5):
             for c in range(5):
                 y = r if k // 2 else 27 + r
                 z = c if k % 2 else 11 + c
-                outgoing[y * 16 + z, 768 + k * 32 + r * 5 + c] = 1
+                outgoing[y * 16 + z, 512 + k * 32 + r * 5 + c] = 1
+    for (y, z), i in EDGE.items():
+        outgoing[y * 16 + z, 640 + i] = 1
     second = np.zeros((9, 256, 256), np.float32)
     back = np.zeros((5, 256, 256), np.float32)
     for dy in range(3):
@@ -108,7 +135,7 @@
     sides = np.zeros((8, 256), np.float32)
     for (y, z), lane in wide.items():
         sides[:4, lane] = (y < 0, y >= 16, z < 0, z >= 8)
-    sixteen = (gather, outgoing, second, back, fold, pool, cot_out, cot_in)
+    sixteen = (inside, nearby, around, outgoing, second, back, fold, pool, cot_out, cot_in)
     return tuple(m.astype(jnp.bfloat16) for m in sixteen) + (sides,)
 
 
@@ -131,6 +158,23 @@
 
 def slope(t):
     return jnp.where(t > 0, jnp.float32(1.0), jnp.float32(0.3))
+
+
+def strip(block, start, width):
+    parts = 128 // width
+    rows = block.shape[0] // parts
+    lane = lax.broadcasted_iota(jnp.int32, (1, 128), 1)
+    packed = jnp.zeros((rows, 128), F32)
+    for j in range(parts):
+        piece = block[rows * j : rows * j + rows]
+        shift = (width * j - start) % 128
+        packed = jnp.where(lane // width == j, pltpu.roll(piece, shift, 1) if shift else piece, packed)
+    return packed
+
+
+def unstrip(packed, start, width, j):
+    shift = (start - width * j) % 128
+    return pltpu.roll(packed, shift, 1) if shift else packed
 
 
 def split(t):
@@ -142,17 +186,17 @@
 CORNERS = ((1, 1), (1, -1), (-1, 1), (-1, -1))
 DIRS = FACES + CORNERS
 XY = tuple((a, b) for a in range(4) for b in range(4) if (a, b) != (0, 0))
-S_RAW, S_COT, S_CORE, S_XY, S_Z, S_AG = 0, 8, 16, 24, 40, 48
+S_RIM, S_CORE, S_XY, S_Z, S_AG, S_FXY, S_FZ = 0, 8, 16, 31, 38, 53, 68
 
 
 def body(
-    vol, k1, w2, cot, gather_h, outgoing_h, second_h, back_h, fold_h, pool_h, cot_out_h, cot_in_h, sides,
-    feat_out, grad_out, first_out, second_out,
-    gather, outgoing, second, back, fold, pool, cot_out, cot_in,
-    rows32, lraw, sy_buf, sz_buf, sc_buf, ry_buf, rz_buf, rc_buf, edge_in,
-    cot_send, cot_recv, x4, x4i, pre1, weights1, forward2, backward2, k1s,
+    vol, k1, w2, cot, inside_h, nearby_h, around_h, outgoing_h, second_h, back_h, fold_h, pool_h, cot_out_h, cot_in_h,
+    sides, feat_out, grad_out, second_out, first_out,
+    inside, nearby, around, outgoing, second, back, fold, pool, cot_out, cot_in,
+    rows32, lraw, y_send, z_send, c_send, y_recv, z_recv, c_recv, edge_a, edge_b, early,
+    x4, x4i, pre1, weights1, forward2, backward2, k1s,
     p2, b2i, b2r, t2i, t2r, spread_i, spread_r, pooled, pg, gshift, bg, t3, g1,
-    total, core_in, xy_in, z_in, final,
+    total, core_in, xy_in, z_in, final, first_part, first_in, first_xy, first_z, first_final,
     local_sem, send_sem, recv_sem,
 ):
     dp, g, s = lax.axis_index("dp"), lax.axis_index("gx"), lax.axis_index("yz")
@@ -167,8 +211,8 @@
         pltpu.make_async_copy(a, b, local_sem.at[i])
         for i, (a, b) in enumerate(
             (
-                (outgoing_h, outgoing), (cot_out_h, cot_out), (fold_h, fold), (pool_h, pool), (cot_in_h, cot_in),
-                (gather_h, gather), (second_h, second), (back_h, back),
+                (outgoing_h, outgoing), (cot_out_h, cot_out), (fold_h, fold), (pool_h, pool), (inside_h, inside),
+                (cot_in_h, cot_in), (nearby_h, nearby), (around_h, around), (second_h, second), (back_h, back),
             )
         )
     ]
@@ -199,40 +243,37 @@
     lraw[0:128, 0:512] = rows32[...].astype(BF16)
     loads[0].wait()
     out = mm(lraw[0:128, 0:512], outgoing[...])
-    sy_buf[0] = (out[:, 0:128] * valid(1, 0)).astype(BF16)
-    sy_buf[1] = (out[:, 128:256] * valid(-1, 0)).astype(BF16)
-    sz_buf[0] = (out[:, 256:512] * valid(0, 1)).astype(BF16)
-    sz_buf[1] = (out[:, 512:768] * valid(0, -1)).astype(BF16)
-    for k, (a, b) in enumerate(CORNERS):
-        packed = jnp.zeros((32, 128), F32)
-        for j in range(4):
-            piece = out[32 * j : 32 * j + 32, 768:896]
-            moved = pltpu.roll(piece, (32 * (j - k)) % 128, 1) if j != k else piece
-            packed = jnp.where(lane // 32 == j, moved, packed)
-        sc_buf[k] = (packed * valid(a, b)).astype(BF16)
     loads[1].wait()
     strips = mm(cot[...], cot_out[...])
     for i, (a, b) in enumerate(DIRS):
-        part = strips[:, 0:128] if a == 0 else strips[:, 128:256]
-        cot_send[i] = (part * valid(a, b)).astype(BF16)
+        ok = valid(a, b)
+        if i < 2:
+            y_send[i, 0:64] = (strip(out[:, 0:128], 64 * i, 64) * ok).astype(BF16)
+            y_send[i, 64:80] = (strip(out[:, 128:256], 16 * i, 16) * ok).astype(BF16)
+            y_send[i, 80:96] = (strip(strips[:, 128:256], 32 - 32 * i, 32) * ok).astype(BF16)
+        elif i < 4:
+            j = i - 2
+            z_send[j, 0:128] = (out[:, 256 + 128 * j : 384 + 128 * j] * ok).astype(BF16)
+            z_send[j, 128:160] = (strip(out[:, 128:256], 32 + 32 * j, 32) * ok).astype(BF16)
+            z_send[j, 160:192] = (strip(strips[:, 0:128], 64 - 64 * j, 64) * ok).astype(BF16)
+        else:
+            j = i - 4
+            c_send[j, 0:32] = (strip(out[:, 512:640], 32 * j, 32) * ok).astype(BF16)
+            c_send[j, 32:48] = (strip(strips[:, 128:256], 32 if a > 0 else 0, 32) * ok).astype(BF16)
 
     pl.semaphore_wait(barrier, len(everyone))
-    raw_copies = []
-    for i in (4, 5, 6, 7, 0, 1, 2, 3):
-        if i >= 4:
-            pair = (sc_buf.at[i - 4], rc_buf.at[i - 4])
-        elif i >= 2:
-            pair = (sz_buf.at[i - 2], rz_buf.at[i - 2])
-        else:
-            pair = (sy_buf.at[i], ry_buf.at[i])
-        copy = remote(pair[0], pair[1], S_RAW + i, near[i])
+    rim_copies = []
+    for i in (4, 5, 6, 7, 2, 3, 0, 1):
+        pair = ((y_send, y_recv), (z_send, z_recv), (c_send, c_recv), (c_send, c_recv))[i // 2]
+        slot = i - 4 if i >= 4 else i % 2
+        copy = remote(pair[0].at[slot], pair[1].at[slot], S_RIM + i, near[i])
         copy.start()
-        raw_copies.append(copy)
-    cot_copies = []
-    for i in range(8):
-        copy = remote(cot_send.at[i], cot_recv.at[i], S_COT + i, near[i])
-        copy.start()
-        cot_copies.append(copy)
+        rim_copies.append(copy)
+    mine = pl.multiple_of(jnp.where(g == 0, 112, 0), 16)
+    early_edge = remote(lraw.at[pl.ds(mine, 16), 0:512], edge_a, S_CORE, other)
+    early_edge.start()
+    core_copies = [early_edge]
+    lraw[0:128, 1152:1280] = out[:, 640:768].astype(BF16)
 
     k1s[...] = jnp.zeros_like(k1s)
     for tap in range(27):
@@ -257,47 +298,71 @@
     far = pl.multiple_of(g * (17 * 64), 64)
     pg[pl.ds(far, 64), :] = jnp.zeros((64, 256), BF16)
     gshift[...] = jnp.zeros_like(gshift)
-    lraw[128:144, :] = jnp.zeros((16, KRAW), BF16)
+    early_edge.wait_recv()
+    first_core = jnp.where(g == 0, jnp.float32(1.0), jnp.float32(0.0))
+    half_row = lax.broadcasted_iota(jnp.int32, (8, 1), 0)
+
+    def beyond(edge):
+        edge = edge.astype(F32)
+        edge = jnp.where(half_row < 4, edge[0:8] * first_core, edge[8:16] * (1.0 - first_core))
+        return jnp.concatenate([edge, jnp.zeros_like(edge)], axis=0).astype(BF16)
+
+    lraw[128:144, 0:512] = beyond(edge_a[...])
     for load in loads[4:]:
         load.wait()
 
-    for copy in raw_copies:
+    def early_step(step, carry):
+        early[step] = mm(lraw[:, 0:512], inside[step])
+        return carry
+
+    lax.fori_loop(0, 8, early_step, 0)
+
+    for copy in rim_copies:
         copy.wait_recv()
-    lraw[0:128, 512:640] = ry_buf[0]
-    lraw[0:128, 640:768] = ry_buf[1]
-    lraw[0:128, 768:1024] = rz_buf[0]
-    lraw[0:128, 1024:1280] = rz_buf[1]
+    for j in range(2):
+        low = unstrip(y_recv[0, 0:64].astype(F32), 0, 64, j)
+        high = unstrip(y_recv[1, 0:64].astype(F32), 64, 64, j)
+        lraw[64 * j : 64 * j + 64, 768:896] = jnp.where(lane < 64, low, high).astype(BF16)
+    lraw[0:128, 896:1024] = z_recv[0, 0:128]
+    lraw[0:128, 1024:1152] = z_recv[1, 0:128]
+    y_low, y_high = y_recv[0, 64:80].astype(F32), y_recv[1, 64:80].astype(F32)
+    for j in range(8):
+        at = slice(128 + 16 * (j % 2), 144 + 16 * (j % 2))
+        z_low, z_high = z_recv[0, at].astype(F32), z_recv[1, at].astype(F32)
+        block = jnp.where(lane < 16, unstrip(y_low, 0, 16, j), unstrip(y_high, 16, 16, j))
+        block = jnp.where(lane < 32, block, unstrip(z_low, 32, 32, j // 2))
+        block = jnp.where(lane < 64, block, unstrip(z_high, 64, 32, j // 2))
+        lraw[16 * j : 16 * j + 16, 512:640] = block.astype(BF16)
     for j in range(4):
-        corner = jnp.zeros((32, 128), F32)
+        block = jnp.zeros((32, 128), F32)
         for k in range(4):
-            piece = rc_buf[k].astype(F32)
-            moved = pltpu.roll(piece, (32 * (k - j)) % 128, 1) if j != k else piece
-            corner = jnp.where(lane // 32 == k, moved, corner)
-        lraw[32 * j : 32 * j + 32, 1280:1408] = corner.astype(BF16)
-    mine = pl.multiple_of(jnp.where(g == 0, 112, 0), 16)
-    copy = remote(lraw.at[pl.ds(mine, 16), :], edge_in, S_CORE, other)
+            block = jnp.where(lane // 32 == k, unstrip(c_recv[k, 0:32].astype(F32), 32 * k, 32, j), block)
+        lraw[32 * j : 32 * j + 32, 640:768] = block.astype(BF16)
+    copy = remote(lraw.at[pl.ds(mine, 16), 512:1280], edge_b, S_CORE + 1, other)
     copy.start()
-    core_copies = [copy]
+    core_copies.append(copy)
     copy.wait_recv()
-    first_core = jnp.where(g == 0, jnp.float32(1.0), jnp.float32(0.0))
-    edge = edge_in[...].astype(F32)
-    half_row = lax.broadcasted_iota(jnp.int32, (8, 1), 0)
-    edge = jnp.where(half_row < 4, edge[0:8] * first_core, edge[8:16] * (1.0 - first_core))
-    lraw[128:144, :] = jnp.concatenate([edge, jnp.zeros_like(edge)], axis=0).astype(BF16)
-
-    def gather_step(tap, carry):
-        got = mm(lraw[...], gather[tap])
+    lraw[128:144, 512:1280] = beyond(edge_b[...])
+
+    def gather_step(step, carry):
+        mid = mm(lraw[:, 512:768], nearby[step]) + early[step]
+        rim = mm(lraw[:, 512:1280], around[step])
         low = half_row < 4
-        at = pl.multiple_of(tap * 16, 16)
-        for x in range(16):
-            after = got[8 * x + 8 : 8 * x + 16]
-            before = got[8 * x - 8 : 8 * x] if x else got[128:136]
-            block = jnp.concatenate([got[8 * x : 8 * x + 8], jnp.where(low, after, before)], axis=0).astype(BF16)
-            x4[x, pl.ds(at, 16), :] = block
-            x4i[pl.ds(at, 16), 128 * x : 128 * x + 128] = block[:, 0:128]
+        for shift in range(2):
+            at = pl.multiple_of(step * 32 + shift * 16, 16)
+            lanes = slice(128 * shift, 128 * shift + 128)
+            for x in range(16):
+                for got, side in ((mid[:, lanes], 0), (rim[:, lanes], 1)):
+                    after = got[8 * x + 8 : 8 * x + 16]
+                    before = got[8 * x - 8 : 8 * x] if x else got[128:136]
+                    block = jnp.concatenate([got[8 * x : 8 * x + 8], jnp.where(low, after, before)], axis=0)
+                    block = block.astype(BF16)
+                    x4[x, pl.ds(at, 16), 128 * side : 128 * side + 128] = block
+                    if side == 0:
+                        x4i[pl.ds(at, 16), 128 * x : 128 * x + 128] = block
         return carry
 
-    lax.fori_loop(0, 16, gather_step, 0)
+    lax.fori_loop(0, 8, gather_step, 0)
 
     def flag(test):
         return jnp.where(test, jnp.float32(1.0), jnp.float32(0.0))
@@ -320,21 +385,23 @@
     lax.fori_loop(0, 16, first_layer, 0)
     near_src = pl.multiple_of(jnp.where(g == 0, 16 * 32, 32), 32)
     near_dst = pl.multiple_of(jnp.where(g == 0, 0, 17 * 32), 32)
-    copy = remote(p2.at[pl.ds(near_src, 32), :], p2.at[pl.ds(near_dst, 32), :], S_CORE + 1, other)
+    copy = remote(p2.at[pl.ds(near_src, 32), :], p2.at[pl.ds(near_dst, 32), :], S_CORE + 2, other)
     copy.start()
     core_copies.append(copy)
 
-    for cot_copy in cot_copies:
-        cot_copy.wait_recv()
-    down, up, left, right = (cot_recv[i] for i in range(4))
-    zs = jnp.where(lane >= 64, left.astype(F32), right.astype(F32))
-    ys = jnp.where(lane >= 32, down.astype(F32), up.astype(F32))
+    zs, ys, cs = [], [], []
+    for j in range(2):
+        low, high = z_recv[0, 160:192].astype(F32), z_recv[1, 160:192].astype(F32)
+        zs.append(jnp.where(lane >= 64, unstrip(low, 64, 64, j), unstrip(high, 0, 64, j)))
     late = lane % 4 == 3
-    cs = jnp.where(
-        lane >= 32,
-        jnp.where(late, cot_recv[4].astype(F32), cot_recv[5].astype(F32)),
-        jnp.where(late, cot_recv[6].astype(F32), cot_recv[7].astype(F32)),
-    )
+    for j in range(4):
+        low, high = y_recv[0, 80:96].astype(F32), y_recv[1, 80:96].astype(F32)
+        ys.append(jnp.where(lane >= 32, unstrip(low, 32, 32, j), unstrip(high, 0, 32, j)))
+        ends = [unstrip(c_recv[k, 32:48].astype(F32), 32 if k < 2 else 0, 32, j) for k in range(4)]
+        cs.append(
+            jnp.where(lane >= 32, jnp.where(late, ends[0], ends[1]), jnp.where(late, ends[2], ends[3]))
+        )
+    zs, ys, cs = (jnp.concatenate(parts, axis=0) for parts in (zs, ys, cs))
     rim = jnp.concatenate([zs, ys, cs], axis=1).astype(BF16)
     spread_r[...] = mm(rim, cot_in[...])
 
@@ -379,7 +446,7 @@
         pooled[half // 4, 64:128, at] = low
     near_src = pl.multiple_of(jnp.where(g == 0, 16 * 64, 64), 64)
     near_dst = pl.multiple_of(jnp.where(g == 0, 0, 17 * 64), 64)
-    copy = remote(pg.at[pl.ds(near_src, 64), :], pg.at[pl.ds(near_dst, 64), :], S_CORE + 2, other)
+    copy = remote(pg.at[pl.ds(near_src, 64), :], pg.at[pl.ds(near_dst, 64), :], S_CORE + 3, other)
     copy.start()
     core_copies.append(copy)
     for half in range(2):
@@ -390,7 +457,12 @@
     total[0:288, :] = grad2[:, 0:128]
     total[288:432, 0:64] = grad2[0:144, 128:192]
     total[288:432, 64:128] = grad2[144:288, 128:192]
-    total[464:512, :] = jnp.zeros((48, 128), F32)
+    total[432:512, :] = jnp.zeros((80, 128), F32)
+    mine = pl.multiple_of(g * 256, 256)
+    theirs = pl.multiple_of((1 - g) * 256, 256)
+    halves = remote(total.at[pl.ds(theirs, 256), :], core_in, S_CORE + 4, other)
+    halves.start()
+    core_copies.append(halves)
     copy.wait_recv()
 
     def back_step(step, carry):
@@ -403,6 +475,16 @@
         return carry
 
     lax.fori_loop(0, 5, back_step, 0)
+
+    halves.wait_recv()
+    core_in[...] = core_in[...] + total[pl.ds(mine, 256), :]
+    xy_copies = []
+    for i, (a, b) in enumerate(XY):
+        piece = ((dp + a) % 4) * 4 + (yi + b) % 4
+        source = core_in.at[pl.ds(pl.multiple_of(piece * 16, 16), 16), :]
+        copy = remote(source, xy_in.at[i], S_XY + i, flat[i])
+        copy.start()
+        xy_copies.append(copy)
 
     def back_layer(chunk, carry):
         at = pl.ds(pl.multiple_of(chunk * 256, 256), 256)
@@ -427,22 +509,15 @@
     for phase in range(8):
         high, low = split(wide[32 * phase : 32 * phase + 32])
         partial = partial + mm_nt(jnp.concatenate([high, low], axis=0), fold[:, 256 * phase : 256 * phase + 256])
-    total[432:464, :] = partial[0:32] + partial[32:64]
-
-    mine = pl.multiple_of(g * 256, 256)
-    theirs = pl.multiple_of((1 - g) * 256, 256)
-    copy = remote(total.at[pl.ds(theirs, 256), :], core_in, S_CORE + 3, other)
-    copy.start()
-    copy.wait()
-    core_in[...] = core_in[...] + total[pl.ds(mine, 256), :]
-    xy_copies = []
-    for i, (a, b) in enumerate(XY):
-        piece = ((dp + a) % 4) * 4 + (yi + b) % 4
-        source = core_in.at[pl.ds(pl.multiple_of(piece * 16, 16), 16), :]
-        copy = remote(source, xy_in.at[i], S_XY + i, flat[i])
-        copy.start()
-        xy_copies.append(copy)
-    place = pl.multiple_of((dp * 4 + yi) * 16, 16)
+    first_part[...] = partial[0:32] + partial[32:64]
+
+    my_half = pl.multiple_of(g * 16, 16)
+    their_half = pl.multiple_of((1 - g) * 16, 16)
+    swap = remote(first_part.at[pl.ds(their_half, 16), :], first_in, S_CORE + 5, other)
+    swap.start()
+    core_copies.append(swap)
+    spot = dp * 4 + yi
+    place = pl.multiple_of(spot * 16, 16)
     part = core_in[pl.ds(place, 16), :]
     for i, copy in enumerate(xy_copies):
         copy.wait_recv()
@@ -453,6 +528,13 @@
         copy = remote(z_in.at[zi], z_in.at[zi], S_Z + k, tall[k])
         copy.start()
         z_copies.append(copy)
+    swap.wait_recv()
+    first_xy[spot] = first_in[...] + first_part[pl.ds(my_half, 16), :]
+    fxy_copies = []
+    for i in range(15):
+        copy = remote(first_xy.at[spot], first_xy.at[spot], S_FXY + i, flat[i])
+        copy.start()
+        fxy_copies.append(copy)
     for copy in z_copies:
         copy.wait_recv()
     part = z_in[0]
@@ -465,40 +547,68 @@
         copy = remote(final.at[rows, :], final.at[rows, :], S_AG + i, flat[i])
         copy.start()
         ag_copies.append(copy)
+    for copy in fxy_copies:
+        copy.wait_recv()
+    part = first_xy[0]
+    for k in range(1, 16):
+        part = part + first_xy[k]
+    first_z[zi] = part
+    fz_copies = []
+    for k in range(7):
+        copy = remote(first_z.at[zi], first_z.at[zi], S_FZ + k, tall[k])
+        copy.start()
+        fz_copies.append(copy)
     for copy in ag_copies:
         copy.wait_recv()
     half = pl.ds(mine, 256)
-    copy = remote(final.at[half, :], final.at[half, :], S_CORE + 4, other)
+    joined = remote(final.at[half, :], final.at[half, :], S_CORE + 6, other)
+    joined.start()
+    core_copies.append(joined)
+    for copy in fz_copies:
+        copy.wait_recv()
+    part = first_z[0]
+    for k in range(1, 8):
+        part = part + first_z[k]
+    half = pl.ds(my_half, 16)
+    first_final[half, :] = part
+    copy = remote(first_final.at[half, :], first_final.at[half, :], S_CORE + 7, other)
     copy.start()
     core_copies.append(copy)
+    joined.wait_recv()
+    second_out[...] = final[0:432, :]
     copy.wait_recv()
-
+    first_out[...] = first_final[...]
+
+    for copy in rim_copies + core_copies + xy_copies + z_copies + ag_copies + fxy_copies + fz_copies:
+        copy.wait_send()
+
+
+def arrange(feat, grad, second, first, feat_out, grad_out, first_out, second_out):
+    feat_out[...] = feat[...]
+    grad_out[...] = grad[...]
     for a in range(9):
         at = slice(32 * a, 32 * a + 32)
-        second_out[a] = final[at, 0:64]
-        second_out[9 + a] = final[at, 64:128]
+        second_out[a] = second[at, 0:64]
+        second_out[9 + a] = second[at, 64:128]
     for a in range(36):
         row = 288 + (8 * a) % 144
         lanes = slice(0, 64) if a < 18 else slice(64, 128)
-        second_out[18 + a // 4, 8 * (a % 4) : 8 * (a % 4) + 8, :] = final[row : row + 8, lanes]
-    flipped = final[432:464, :].T
+        second_out[18 + a // 4, 8 * (a % 4) : 8 * (a % 4) + 8, :] = second[row : row + 8, lanes]
+    flipped = first[...].T
     for tap in range(27):
         first_out[tap] = flipped[4 * tap : 4 * tap + 4, :]
-
-    for copy in raw_copies + cot_copies + core_copies + xy_copies + z_copies + ag_copies:
-        copy.wait_send()
 
 
 def on_device(volumes, first_kernel, second_kernel, cotangent):
     consts = matrices()
     here = pl.BlockSpec(memory_space=pltpu.VMEM)
-    there = pl.BlockSpec(memory_space=pl.ANY)
+    there = pl.BlockSpec(memory_space=pltpu.HBM)
     vmem = pltpu.VMEM
-    scratch = [vmem(m.shape, BF16) for m in consts[:8]] + [
+    scratch = [vmem(m.shape, BF16) for m in consts[:-1]] + [
         vmem((128, 512), F32), vmem((144, KRAW), BF16),
-        vmem((2, 128, 128), BF16), vmem((2, 128, 256), BF16), vmem((4, 32, 128), BF16),
-        vmem((2, 128, 128), BF16), vmem((2, 128, 256), BF16), vmem((4, 32, 128), BF16), vmem((16, KRAW), BF16),
-        vmem((8, 64, 128), BF16), vmem((8, 64, 128), BF16),
+        vmem((2, 96, 128), BF16), vmem((2, 192, 128), BF16), vmem((4, 48, 128), BF16),
+        vmem((2, 96, 128), BF16), vmem((2, 192, 128), BF16), vmem((4, 48, 128), BF16),
+        vmem((16, 512), BF16), vmem((16, 768), BF16), vmem((8, 144, 256), F32),
         vmem((16, 256, 256), BF16), vmem((256, 2048), BF16), vmem((16, 256, 128), F32),
         vmem((256, 256), BF16), vmem((192, 288), BF16), vmem((96, 576), BF16), vmem((128, 32), F32),
         vmem((576, 256), BF16), vmem((288, 2304), BF16), vmem((288, 2304), BF16),
@@ -506,21 +616,22 @@
         vmem((2, 128, 512), BF16), vmem((1152, 256), BF16), vmem((192, 2304), BF16),
         vmem((640, 2304), BF16), vmem((96, 2304), F32), vmem((256, 2048), BF16),
         vmem((512, 128), F32), vmem((256, 128), F32), vmem((15, 16, 128), F32), vmem((8, 16, 128), F32), vmem((512, 128), F32),
-        pltpu.SemaphoreType.DMA((8,)), pltpu.SemaphoreType.DMA((63,)), pltpu.SemaphoreType.DMA((63,)),
+        vmem((32, 128), F32), vmem((16, 128), F32), vmem((16, 16, 128), F32), vmem((8, 16, 128), F32), vmem((32, 128), F32),
+        pltpu.SemaphoreType.DMA((10,)), pltpu.SemaphoreType.DMA((75,)), pltpu.SemaphoreType.DMA((75,)),
     ]
-    features, act_grad, first_grad, second_grad = pl.pallas_call(
+    parts = pl.pallas_call(
         body,
         out_shape=(
             jax.ShapeDtypeStruct((64, 256), BF16),
             jax.ShapeDtypeStruct((512, 128), F32),
-            jax.ShapeDtypeStruct((27, 4, 32), F32),
-            jax.ShapeDtypeStruct((27, 32, 64), F32),
+            jax.ShapeDtypeStruct((432, 128), F32),
+            jax.ShapeDtypeStruct((32, 128), F32),
         ),
-        in_specs=[here] * 4 + [there] * 8 + [here],
+        in_specs=[here] * 4 + [there] * 10 + [here],
         out_specs=(here,) * 4,
         scratch_shapes=scratch,
         compiler_params=pltpu.CompilerParams(
-            collective_id=0, has_side_effects=True, vmem_limit_bytes=56 * 1024 * 1024
+            collective_id=0, has_side_effects=True, vmem_limit_bytes=60 * 1024 * 1024
         ),
     )(
         volumes.reshape(4, 16384),
@@ -529,6 +640,17 @@
         cotangent.reshape(64, 256),
         *(jnp.asarray(m) for m in consts),
     )
+    features, act_grad, first_grad, second_grad = pl.pallas_call(
+        arrange,
+        out_shape=(
+            jax.ShapeDtypeStruct((64, 256), BF16),
+            jax.ShapeDtypeStruct((512, 128), F32),
+            jax.ShapeDtypeStruct((27, 4, 32), F32),
+            jax.ShapeDtypeStruct((27, 32, 64), F32),
+        ),
+        in_specs=[here] * 4,
+        out_specs=(here,) * 4,
+    )(*parts)
     return (
         features.reshape(1, 64, 1, 1, 256),
         act_grad.reshape(1, 32, 1, 1, 2048),

time: 67.1 us -> 54.8 us (0.82)
  local copies, waits for them, and re-layouts: 6.29 us -> 0 us
  Pallas kernels: 59.9 us -> 54.1 us
    pallas_call x1, Pallas kernels: 59.9 us -> 52.1 us  [on_device(): pl.pallas_call(body, out_shape=(jax.ShapeDtypeStruct((64, 256), BF16), ja...]
    unnamed x4 -> x0, local copies, waits for them, and re-layouts: 6.29 us -> none
    pallas_call x0 -> x1, Pallas kernels: none -> 2.01 us  [on_device(): pl.pallas_call(arrange, out_shape=(jax.ShapeDtypeStruct((64, 256), BF16),...]
where the time goes in v2:
time: 54.8 us; the launch traced here: 54.7 us
  Pallas kernels  54.1 us (99%)
  between operations  0.64 us (1%)
    pallas_call x1, Pallas kernels, on_device(): pl.pallas_call(body, out_shape=(jax.ShapeDtypeStruct((64, 256), BF16), ja...  52.1 us
    pallas_call x1, Pallas kernels, on_device(): pl.pallas_call(arrange, out_shape=(jax.ShapeDtypeStruct((64, 256), BF16),...  2.01 us

profile of v2, /device:TPU:1, one launch (start us, length us, event | category | flops | bytes accessed | tf_op | source)
XLA Modules:
  0.0 54.7 jit_solution(17905344265272777610)
XLA Ops:
  0.6 52.1 %shard_map.174 = (bf16[64,256]{1,0:T(8,128)(2,1)}, f32[512,128]{1,0:T(8,128)}, f32[432,128]{1,0:T(8,128)}, f32[32,128]{1,0:T(8,128)}) custom-call(bf16[4,16384]{1,0:T(4,128)(2,1)} %bitcast.17, bf16[27,4,32]{2,1,0:T(4,128)(2,1)} %bitcast.19, bf16[27,32,64]{2,1,0:T(8,128)(2,1)} %bitcast.16, bf16[64,256]{1,0:T(8,128)(2,1)} %bitcast.18, ...), custom_call_target="tpu_custom_call" | custom-call | tf_op jit(solution)/shard_map/pallas_call | solution.py:622
  52.7 2.0 %shard_map.175 = (bf16[64,256]{1,0:T(8,128)(2,1)}, f32[512,128]{1,0:T(8,128)}, f32[27,4,32]{2,1,0:T(4,128)}, f32[27,32,64]{2,1,0:T(8,128)}) custom-call(bf16[64,256]{1,0:T(8,128)(2,1)} %get-tuple-element.12.feat, f32[512,128]{1,0:T(8,128)} %get-tuple-element.13.grad, f32[432,128]{1,0:T(8,128)} %get-tuple-element.14.second, f32[32,128]{1,0:T(8,128)} %get-tuple-element.15.first), custom_call_target="tpu_custom_call" | custom-call | tf_op jit(solution)/shard_map/pallas_call | solution.py:643

commit v3 on v2

--- a/solution.py
+++ b/solution.py
@@ -190,8 +190,9 @@
 
 
 def body(
-    vol, k1, w2, cot, inside_h, nearby_h, around_h, outgoing_h, second_h, back_h, fold_h, pool_h, cot_out_h, cot_in_h,
-    sides, feat_out, grad_out, second_out, first_out,
+    vol_h, k1_h, w2_h, cot_h, inside_h, nearby_h, around_h, outgoing_h, second_h, back_h, fold_h, pool_h, cot_out_h, cot_in_h,
+    sides_h, feat_out, grad_out, second_out, first_out,
+    vol, k1, w2, cot, sides, feat, grads,
     inside, nearby, around, outgoing, second, back, fold, pool, cot_out, cot_in,
     rows32, lraw, y_send, z_send, c_send, y_recv, z_recv, c_recv, edge_a, edge_b, early,
     x4, x4i, pre1, weights1, forward2, backward2, k1s,
@@ -211,8 +212,9 @@
         pltpu.make_async_copy(a, b, local_sem.at[i])
         for i, (a, b) in enumerate(
             (
-                (outgoing_h, outgoing), (cot_out_h, cot_out), (fold_h, fold), (pool_h, pool), (inside_h, inside),
-                (cot_in_h, cot_in), (nearby_h, nearby), (around_h, around), (second_h, second), (back_h, back),
+                (vol_h, vol), (outgoing_h, outgoing), (cot_h, cot), (cot_out_h, cot_out), (k1_h, k1), (w2_h, w2),
+                (fold_h, fold), (pool_h, pool), (inside_h, inside), (cot_in_h, cot_in), (nearby_h, nearby),
+                (around_h, around), (second_h, second), (back_h, back), (sides_h, sides),
             )
         )
     ]
@@ -238,12 +240,14 @@
 
     lane = lax.broadcasted_iota(jnp.int32, (1, 128), 1)
 
+    loads[0].wait()
     for x in range(32):
         rows32[4 * x : 4 * x + 4, :] = vol[:, x * 512 : (x + 1) * 512].astype(F32)
     lraw[0:128, 0:512] = rows32[...].astype(BF16)
-    loads[0].wait()
+    loads[1].wait()
     out = mm(lraw[0:128, 0:512], outgoing[...])
-    loads[1].wait()
+    loads[2].wait()
+    loads[3].wait()
     strips = mm(cot[...], cot_out[...])
     for i, (a, b) in enumerate(DIRS):
         ok = valid(a, b)
@@ -275,10 +279,12 @@
     core_copies = [early_edge]
     lraw[0:128, 1152:1280] = out[:, 640:768].astype(BF16)
 
+    loads[4].wait()
+    loads[5].wait()
     k1s[...] = jnp.zeros_like(k1s)
     for tap in range(27):
         k1s[4 * tap : 4 * tap + 4, :] = k1[tap].astype(F32)
-    loads[2].wait()
+    loads[6].wait()
     k1t = mm_nt(identity(32), k1s[...].astype(BF16)).astype(BF16)
     for phase in range(8):
         weights1[32 * phase : 32 * phase + 32, :] = mm(k1t, fold[:, 256 * phase : 256 * phase + 256]).astype(BF16)
@@ -290,7 +296,7 @@
             both = jnp.concatenate([w2[9 * x + a].astype(F32), w2[9 * x + a + 1].astype(F32)], axis=1)
             backward2[32 * x : 32 * x + 32, 64 * a : 64 * a + 128] = both.astype(BF16)
         backward2[32 * x : 32 * x + 32, 512:576] = w2[9 * x + 8]
-    loads[3].wait()
+    loads[7].wait()
     for half in range(2):
         spread_i[:, 512 * half : 512 * half + 512] = mm_nt(cot[:, 128 * half : 128 * half + 128], pool[...])
     far = pl.multiple_of(g * (17 * 32), 32)
@@ -308,14 +314,14 @@
         return jnp.concatenate([edge, jnp.zeros_like(edge)], axis=0).astype(BF16)
 
     lraw[128:144, 0:512] = beyond(edge_a[...])
-    for load in loads[4:]:
+    for load in loads[8:]:
         load.wait()
 
     def early_step(step, carry):
         early[step] = mm(lraw[:, 0:512], inside[step])
         return carry
 
-    lax.fori_loop(0, 8, early_step, 0)
+    lax.fori_loop(0, 8, early_step, 0, unroll=True)
 
     for copy in rim_copies:
         copy.wait_recv()
@@ -362,7 +368,7 @@
                         x4i[pl.ds(at, 16), 128 * x : 128 * x + 128] = block
         return carry
 
-    lax.fori_loop(0, 8, gather_step, 0)
+    lax.fori_loop(0, 8, gather_step, 0, unroll=True)
 
     def flag(test):
         return jnp.where(test, jnp.float32(1.0), jnp.float32(0.0))
@@ -382,7 +388,7 @@
         p2[pl.ds(pl.multiple_of(32 * x + 32, 32), 32), :] = (act * scale).astype(BF16)
         return carry
 
-    lax.fori_loop(0, 16, first_layer, 0)
+    lax.fori_loop(0, 16, first_layer, 0, unroll=True)
     near_src = pl.multiple_of(jnp.where(g == 0, 16 * 32, 32), 32)
     near_dst = pl.multiple_of(jnp.where(g == 0, 0, 17 * 32), 32)
     copy = remote(p2.at[pl.ds(near_src, 32), :], p2.at[pl.ds(near_dst, 32), :], S_CORE + 2, other)
@@ -416,7 +422,7 @@
             b2r[pl.ds(at, 32), 128 * x : 128 * x + 128] = block[:, 128:256]
         return carry
 
-    lax.fori_loop(0, 9, shift_step, 0)
+    lax.fori_loop(0, 9, shift_step, 0, unroll=True)
 
     def second_layer(chunk, carry):
         at = pl.ds(pl.multiple_of(chunk * 256, 256), 256)
@@ -424,7 +430,7 @@
         t2r[:, at] = mm(forward2[...], b2r[:, at])
         return carry
 
-    lax.fori_loop(0, 9, second_layer, 0)
+    lax.fori_loop(0, 9, second_layer, 0, unroll=True)
 
     for half in range(8):
         lifted = spread_i[:, 128 * half : 128 * half + 128] * 0.125
@@ -451,7 +457,9 @@
     core_copies.append(copy)
     for half in range(2):
         sums = mm(pooled[half], pool[...])
-        feat_out[:, 128 * half : 128 * half + 128] = ((sums[0:64] + sums[64:128]) * 0.125).astype(BF16)
+        feat[:, 128 * half : 128 * half + 128] = ((sums[0:64] + sums[64:128]) * 0.125).astype(BF16)
+    stores = [pltpu.make_async_copy(feat, feat_out, local_sem.at[15])]
+    stores[0].start()
 
     grad2 = mm_nt(b2i[...], gshift[...])
     total[0:288, :] = grad2[:, 0:128]
@@ -474,7 +482,7 @@
             bg[pl.ds(at + 64, 64), 128 * x : 128 * x + 128] = block[:, 128:256]
         return carry
 
-    lax.fori_loop(0, 5, back_step, 0)
+    lax.fori_loop(0, 5, back_step, 0, unroll=True)
 
     halves.wait_recv()
     core_in[...] = core_in[...] + total[pl.ds(mine, 256), :]
@@ -491,7 +499,7 @@
         t3[:, at] = mm(backward2[...], bg[0:576, at])
         return carry
 
-    lax.fori_loop(0, 9, back_layer, 0)
+    lax.fori_loop(0, 9, back_layer, 0, unroll=True)
 
     for x in range(16):
         grad = (
@@ -499,11 +507,13 @@
             + t3[32:64, 128 * (x + 1) : 128 * (x + 2)]
             + t3[64:96, 128 * x : 128 * (x + 1)]
         )
-        grad_out[pl.ds(x, 32, stride=16), :] = grad
+        grads[pl.ds(x, 32, stride=16), :] = grad
         eighth = grad * 0.125
         for phase in range(8):
             at = slice(32 * phase, 32 * phase + 32)
             g1[at, 128 * x : 128 * x + 128] = (eighth * slope(pre1[x, at, :])).astype(BF16)
+    stores.append(pltpu.make_async_copy(grads, grad_out, local_sem.at[16]))
+    stores[1].start()
     wide = mm_nt(g1[...], x4i[...])
     partial = jnp.zeros((64, 128), F32)
     for phase in range(8):
@@ -575,9 +585,13 @@
     copy.start()
     core_copies.append(copy)
     joined.wait_recv()
-    second_out[...] = final[0:432, :]
+    stores.append(pltpu.make_async_copy(final.at[0:432, :], second_out, local_sem.at[17]))
+    stores[2].start()
     copy.wait_recv()
-    first_out[...] = first_final[...]
+    stores.append(pltpu.make_async_copy(first_final, first_out, local_sem.at[18]))
+    stores[3].start()
+    for store in stores:
+        store.wait()
 
     for copy in rim_copies + core_copies + xy_copies + z_copies + ag_copies + fxy_copies + fz_copies:
         copy.wait_send()
@@ -604,7 +618,10 @@
     here = pl.BlockSpec(memory_space=pltpu.VMEM)
     there = pl.BlockSpec(memory_space=pltpu.HBM)
     vmem = pltpu.VMEM
-    scratch = [vmem(m.shape, BF16) for m in consts[:-1]] + [
+    scratch = [
+        vmem((4, 16384), BF16), vmem((27, 4, 32), BF16), vmem((27, 32, 64), BF16), vmem((64, 256), BF16), vmem((8, 256), F32),
+        vmem((64, 256), BF16), vmem((512, 128), F32),
+    ] + [vmem(m.shape, BF16) for m in consts[:-1]] + [
         vmem((128, 512), F32), vmem((144, KRAW), BF16),
         vmem((2, 96, 128), BF16), vmem((2, 192, 128), BF16), vmem((4, 48, 128), BF16),
         vmem((2, 96, 128), BF16), vmem((2, 192, 128), BF16), vmem((4, 48, 128), BF16),
@@ -617,7 +634,7 @@
         vmem((640, 2304), BF16), vmem((96, 2304), F32), vmem((256, 2048), BF16),
         vmem((512, 128), F32), vmem((256, 128), F32), vmem((15, 16, 128), F32), vmem((8, 16, 128), F32), vmem((512, 128), F32),
         vmem((32, 128), F32), vmem((16, 128), F32), vmem((16, 16, 128), F32), vmem((8, 16, 128), F32), vmem((32, 128), F32),
-        pltpu.SemaphoreType.DMA((10,)), pltpu.SemaphoreType.DMA((75,)), pltpu.SemaphoreType.DMA((75,)),
+        pltpu.SemaphoreType.DMA((19,)), pltpu.SemaphoreType.DMA((75,)), pltpu.SemaphoreType.DMA((75,)),
     ]
     parts = pl.pallas_call(
         body,
@@ -627,8 +644,8 @@
             jax.ShapeDtypeStruct((432, 128), F32),
             jax.ShapeDtypeStruct((32, 128), F32),
         ),
-        in_specs=[here] * 4 + [there] * 10 + [here],
-        out_specs=(here,) * 4,
+        in_specs=[there] * 15,
+        out_specs=(there,) * 4,
         scratch_shapes=scratch,
         compiler_params=pltpu.CompilerParams(
             collective_id=0, has_side_effects=True, vmem_limit_bytes=60 * 1024 * 1024

time: 54.8 us -> 46.6 us (0.85)
  Pallas kernels: 54.1 us -> 45.8 us
    pallas_call x1, Pallas kernels: 52.1 us -> 43.8 us  [on_device(): pl.pallas_call(body, out_shape=(jax.ShapeDtypeStruct((64, 256), BF16), ja...]
where the time goes in v3:
time: 46.6 us; the launch traced here: 46.5 us
  Pallas kernels  45.8 us (98%)
  between operations  0.64 us (1%)
    pallas_call x1, Pallas kernels, on_device(): pl.pallas_call(body, out_shape=(jax.ShapeDtypeStruct((64, 256), BF16), ja...  43.8 us
    pallas_call x1, Pallas kernels, on_device(): pl.pallas_call(arrange, out_shape=(jax.ShapeDtypeStruct((64, 256), BF16),...  2.01 us

profile of v3, /device:TPU:1, one launch (start us, length us, event | category | flops | bytes accessed | tf_op | source)
XLA Modules:
  0.0 46.5 jit_solution(5251766402860078999)
XLA Ops:
  0.6 43.8 %shard_map.174 = (bf16[64,256]{1,0:T(8,128)(2,1)}, f32[512,128]{1,0:T(8,128)}, f32[432,128]{1,0:T(8,128)}, f32[32,128]{1,0:T(8,128)}) custom-call(bf16[4,16384]{1,0:T(4,128)(2,1)} %bitcast.17, bf16[27,4,32]{2,1,0:T(4,128)(2,1)} %bitcast.19, bf16[27,32,64]{2,1,0:T(8,128)(2,1)} %bitcast.16, bf16[64,256]{1,0:T(8,128)(2,1)} %bitcast.18, ...), custom_call_target="tpu_custom_call" | custom-call | tf_op jit(solution)/shard_map/pallas_call | solution.py:639
  44.4 2.0 %shard_map.175 = (bf16[64,256]{1,0:T(8,128)(2,1)}, f32[512,128]{1,0:T(8,128)}, f32[27,4,32]{2,1,0:T(4,128)}, f32[27,32,64]{2,1,0:T(8,128)}) custom-call(bf16[64,256]{1,0:T(8,128)(2,1)} %get-tuple-element.12.feat, f32[512,128]{1,0:T(8,128)} %get-tuple-element.13.grad, f32[432,128]{1,0:T(8,128)} %get-tuple-element.14.second, f32[32,128]{1,0:T(8,128)} %get-tuple-element.15.first), custom_call_target="tpu_custom_call" | custom-call | tf_op jit(solution)/shard_map/pallas_call | solution.py:660

commit v4 on v3

--- a/solution.py
+++ b/solution.py
@@ -185,7 +185,11 @@
 FACES = ((1, 0), (-1, 0), (0, 1), (0, -1))
 CORNERS = ((1, 1), (1, -1), (-1, 1), (-1, -1))
 DIRS = FACES + CORNERS
-XY = tuple((a, b) for a in range(4) for b in range(4) if (a, b) != (0, 0))
+XY = sorted(
+    ((a, b) for a in range(4) for b in range(4) if (a, b) != (0, 0)),
+    key=lambda p: -min(p[0], 4 - p[0]) - min(p[1], 4 - p[1]),
+)
+TALL = (4, 3, 5, 2, 6, 1, 7)
 S_RIM, S_CORE, S_XY, S_Z, S_AG, S_FXY, S_FZ = 0, 8, 16, 31, 38, 53, 68
 
 
@@ -206,7 +210,7 @@
     other = (dp, 1 - g, s)
     near = [(dp, g, ((by + a) % PY) * PZ + (bz + b) % PZ) for a, b in DIRS]
     flat = [((dp + a) % 4, g, zi * NY + (yi + b) % NY) for a, b in XY]
-    tall = [(dp, g, ((zi + k) % 8) * NY + yi) for k in range(1, 8)]
+    tall = [(dp, g, ((zi + k) % 8) * NY + yi) for k in TALL]
 
     loads = [
         pltpu.make_async_copy(a, b, local_sem.at[i])
@@ -332,21 +336,30 @@
     lraw[0:128, 896:1024] = z_recv[0, 0:128]
     lraw[0:128, 1024:1152] = z_recv[1, 0:128]
     y_low, y_high = y_recv[0, 64:80].astype(F32), y_recv[1, 64:80].astype(F32)
-    for j in range(8):
+    def fill_inner(j):
         at = slice(128 + 16 * (j % 2), 144 + 16 * (j % 2))
         z_low, z_high = z_recv[0, at].astype(F32), z_recv[1, at].astype(F32)
         block = jnp.where(lane < 16, unstrip(y_low, 0, 16, j), unstrip(y_high, 16, 16, j))
         block = jnp.where(lane < 32, block, unstrip(z_low, 32, 32, j // 2))
         block = jnp.where(lane < 64, block, unstrip(z_high, 64, 32, j // 2))
         lraw[16 * j : 16 * j + 16, 512:640] = block.astype(BF16)
-    for j in range(4):
+    def fill_corner(j):
         block = jnp.zeros((32, 128), F32)
         for k in range(4):
             block = jnp.where(lane // 32 == k, unstrip(c_recv[k, 0:32].astype(F32), 32 * k, 32, j), block)
         lraw[32 * j : 32 * j + 32, 640:768] = block.astype(BF16)
+
+    for j in (0, 7):
+        fill_inner(j)
+    for j in (0, 3):
+        fill_corner(j)
     copy = remote(lraw.at[pl.ds(mine, 16), 512:1280], edge_b, S_CORE + 1, other)
     copy.start()
     core_copies.append(copy)
+    for j in range(1, 7):
+        fill_inner(j)
+    for j in (1, 2):
+        fill_corner(j)
     copy.wait_recv()
     lraw[128:144, 512:1280] = beyond(edge_b[...])
 
@@ -379,21 +392,23 @@
     )
     scale = (1.0 - outside) * 0.125
 
-    def first_layer(x, carry):
+    def first_layer(x):
         pre = mm(weights1[...], x4[x])
         pre1[x] = pre[:, 0:128]
         act = leaky(pre[0:32])
         for phase in range(1, 8):
             act = act + leaky(pre[32 * phase : 32 * phase + 32])
-        p2[pl.ds(pl.multiple_of(32 * x + 32, 32), 32), :] = (act * scale).astype(BF16)
-        return carry
-
-    lax.fori_loop(0, 16, first_layer, 0, unroll=True)
+        p2[32 * x + 32 : 32 * x + 64, :] = (act * scale).astype(BF16)
+
+    first_layer(0)
+    first_layer(15)
     near_src = pl.multiple_of(jnp.where(g == 0, 16 * 32, 32), 32)
     near_dst = pl.multiple_of(jnp.where(g == 0, 0, 17 * 32), 32)
     copy = remote(p2.at[pl.ds(near_src, 32), :], p2.at[pl.ds(near_dst, 32), :], S_CORE + 2, other)
     copy.start()
     core_copies.append(copy)
+    for x in range(1, 15):
+        first_layer(x)
 
     zs, ys, cs = [], [], []
     for j in range(2):
@@ -432,7 +447,7 @@
 
     lax.fori_loop(0, 9, second_layer, 0, unroll=True)
 
-    for half in range(8):
+    for half in (0, 7, 1, 2, 3, 4, 5, 6):
         lifted = spread_i[:, 128 * half : 128 * half + 128] * 0.125
         lifted_rim = spread_r[:, 128 * half : 128 * half + 128] * 0.125
         pair = jnp.zeros((64, 128), F32)
@@ -450,11 +465,12 @@
         at = slice(128 * (half % 4), 128 * (half % 4) + 128)
         pooled[half // 4, 0:64, at] = high
         pooled[half // 4, 64:128, at] = low
-    near_src = pl.multiple_of(jnp.where(g == 0, 16 * 64, 64), 64)
-    near_dst = pl.multiple_of(jnp.where(g == 0, 0, 17 * 64), 64)
-    copy = remote(pg.at[pl.ds(near_src, 64), :], pg.at[pl.ds(near_dst, 64), :], S_CORE + 3, other)
-    copy.start()
-    core_copies.append(copy)
+        if half == 7:
+            near_src = pl.multiple_of(jnp.where(g == 0, 16 * 64, 64), 64)
+            near_dst = pl.multiple_of(jnp.where(g == 0, 0, 17 * 64), 64)
+            copy = remote(pg.at[pl.ds(near_src, 64), :], pg.at[pl.ds(near_dst, 64), :], S_CORE + 3, other)
+            copy.start()
+            core_copies.append(copy)
     for half in range(2):
         sums = mm(pooled[half], pool[...])
         feat[:, 128 * half : 128 * half + 128] = ((sums[0:64] + sums[64:128]) * 0.125).astype(BF16)
@@ -472,18 +488,6 @@
     halves.start()
     core_copies.append(halves)
     copy.wait_recv()
-
-    def back_step(step, carry):
-        got = mm(pg[...], back[step])
-        at = pl.multiple_of(step * 128, 128)
-        for x in range(18):
-            block = got[64 * x : 64 * x + 64].astype(BF16)
-            bg[pl.ds(at, 64), 128 * x : 128 * x + 128] = block[:, 0:128]
-            bg[pl.ds(at + 64, 64), 128 * x : 128 * x + 128] = block[:, 128:256]
-        return carry
-
-    lax.fori_loop(0, 5, back_step, 0, unroll=True)
-
     halves.wait_recv()
     core_in[...] = core_in[...] + total[pl.ds(mine, 256), :]
     xy_copies = []
@@ -493,6 +497,17 @@
         copy = remote(source, xy_in.at[i], S_XY + i, flat[i])
         copy.start()
         xy_copies.append(copy)
+
+    def back_step(step, carry):
+        got = mm(pg[...], back[step])
+        at = pl.multiple_of(step * 128, 128)
+        for x in range(18):
+            block = got[64 * x : 64 * x + 64].astype(BF16)
+            bg[pl.ds(at, 64), 128 * x : 128 * x + 128] = block[:, 0:128]
+            bg[pl.ds(at + 64, 64), 128 * x : 128 * x + 128] = block[:, 128:256]
+        return carry
+
+    lax.fori_loop(0, 5, back_step, 0, unroll=True)
 
     def back_layer(chunk, carry):
         at = pl.ds(pl.multiple_of(chunk * 256, 256), 256)
@@ -528,6 +543,15 @@
     core_copies.append(swap)
     spot = dp * 4 + yi
     place = pl.multiple_of(spot * 16, 16)
+    swap.wait_recv()
+    first_xy[spot] = first_in[...] + first_part[pl.ds(my_half, 16), :]
+    fxy_copies = []
+    for i in range(15):
+        copy = remote(first_xy.at[spot], first_xy.at[spot], S_FXY + i, flat[i])
+        copy.start()
+        fxy_copies.append(copy)
+    for sent in rim_copies + core_copies[:5]:
+        sent.wait_send()
     part = core_in[pl.ds(place, 16), :]
     for i, copy in enumerate(xy_copies):
         copy.wait_recv()
@@ -538,13 +562,17 @@
         copy = remote(z_in.at[zi], z_in.at[zi], S_Z + k, tall[k])
         copy.start()
         z_copies.append(copy)
-    swap.wait_recv()
-    first_xy[spot] = first_in[...] + first_part[pl.ds(my_half, 16), :]
-    fxy_copies = []
-    for i in range(15):
-        copy = remote(first_xy.at[spot], first_xy.at[spot], S_FXY + i, flat[i])
+    for copy in fxy_copies:
+        copy.wait_recv()
+    part = first_xy[0]
+    for k in range(1, 16):
+        part = part + first_xy[k]
+    first_z[zi] = part
+    fz_copies = []
+    for k in range(7):
+        copy = remote(first_z.at[zi], first_z.at[zi], S_FZ + k, tall[k])
         copy.start()
-        fxy_copies.append(copy)
+        fz_copies.append(copy)
     for copy in z_copies:
         copy.wait_recv()
     part = z_in[0]
@@ -557,17 +585,8 @@
         copy = remote(final.at[rows, :], final.at[rows, :], S_AG + i, flat[i])
         copy.start()
         ag_copies.append(copy)
-    for copy in fxy_copies:
-        copy.wait_recv()
-    part = first_xy[0]
-    for k in range(1, 16):
-        part = part + first_xy[k]
-    first_z[zi] = part
-    fz_copies = []
-    for k in range(7):
-        copy = remote(first_z.at[zi], first_z.at[zi], S_FZ + k, tall[k])
-        copy.start()
-        fz_copies.append(copy)
+    for sent in xy_copies + fxy_copies:
+        sent.wait_send()
     for copy in ag_copies:
         copy.wait_recv()
     half = pl.ds(mine, 256)
@@ -584,6 +603,8 @@
     copy = remote(first_final.at[half, :], first_final.at[half, :], S_CORE + 7, other)
     copy.start()
     core_copies.append(copy)
+    for sent in z_copies + ag_copies + fz_copies:
+        sent.wait_send()
     joined.wait_recv()
     stores.append(pltpu.make_async_copy(final.at[0:432, :], second_out, local_sem.at[17]))
     stores[2].start()
@@ -593,8 +614,8 @@
     for store in stores:
         store.wait()
 
-    for copy in rim_copies + core_copies + xy_copies + z_copies + ag_copies + fxy_copies + fz_copies:
-        copy.wait_send()
+    for sent in core_copies[5:]:
+        sent.wait_send()
 
 
 def arrange(feat, grad, second, first, feat_out, grad_out, first_out, second_out):

time: 46.6 us -> 45 us (0.966)
  Pallas kernels: 45.8 us -> 44.3 us
    pallas_call x1, Pallas kernels: 43.8 us -> 42.3 us  [on_device(): pl.pallas_call(body, out_shape=(jax.ShapeDtypeStruct((64, 256), BF16), ja...]
where the time goes in v4:
time: 45 us; the launch traced here: 44.9 us
  Pallas kernels  44.3 us (98%)
  between operations  0.64 us (1%)
    pallas_call x1, Pallas kernels, on_device(): pl.pallas_call(body, out_shape=(jax.ShapeDtypeStruct((64, 256), BF16), ja...  42.3 us
    pallas_call x1, Pallas kernels, on_device(): pl.pallas_call(arrange, out_shape=(jax.ShapeDtypeStruct((64, 256), BF16),...  2.01 us

profile of v4, /device:TPU:1, one launch (start us, length us, event | category | flops | bytes accessed | tf_op | source)
XLA Modules:
  0.0 44.9 jit_solution(5310037859284891062)
XLA Ops:
  0.6 42.3 %shard_map.174 = (bf16[64,256]{1,0:T(8,128)(2,1)}, f32[512,128]{1,0:T(8,128)}, f32[432,128]{1,0:T(8,128)}, f32[32,128]{1,0:T(8,128)}) custom-call(bf16[4,16384]{1,0:T(4,128)(2,1)} %bitcast.17, bf16[27,4,32]{2,1,0:T(4,128)(2,1)} %bitcast.19, bf16[27,32,64]{2,1,0:T(8,128)(2,1)} %bitcast.16, bf16[64,256]{1,0:T(8,128)(2,1)} %bitcast.18, ...), custom_call_target="tpu_custom_call" | custom-call | tf_op jit(solution)/shard_map/pallas_call | solution.py:660
  42.9 2.0 %shard_map.175 = (bf16[64,256]{1,0:T(8,128)(2,1)}, f32[512,128]{1,0:T(8,128)}, f32[27,4,32]{2,1,0:T(4,128)}, f32[27,32,64]{2,1,0:T(8,128)}) custom-call(bf16[64,256]{1,0:T(8,128)(2,1)} %get-tuple-element.12.feat, f32[512,128]{1,0:T(8,128)} %get-tuple-element.13.grad, f32[432,128]{1,0:T(8,128)} %get-tuple-element.14.second, f32[32,128]{1,0:T(8,128)} %get-tuple-element.15.first), custom_call_target="tpu_custom_call" | custom-call | tf_op jit(solution)/shard_map/pallas_call | solution.py:681

commit v5 on v4

--- a/solution.py
+++ b/solution.py
@@ -94,10 +94,13 @@
             tap = dy * 3 + dz
             for (y, z), lane in ring.items():
                 second[tap, wide[(y + dy - 1, z + dz - 1)], lane] = 1
+                if lane >= 128:
+                    second[tap, wide[(y + dy - 1, z + dz - 1)], lane + 64] = 1
             for y in range(16):
                 for z in range(8):
                     source = ring[(y - dy + 1, z - dz + 1)]
-                    back[tap // 2, source, (tap % 2) * 128 + y * 8 + z] = 1
+                    for place in (source,) if source < 128 else (source, source + 64):
+                        back[tap // 2, place, (tap % 2) * 128 + y * 8 + z] = 1
     fold = np.zeros((128, 2048), np.float32)
     for phase in range(8):
         px, py, pz = phase // 4, phase // 2 % 2, phase % 2
@@ -132,6 +135,7 @@
             else:
                 source = 256 + x * 4 + (3 if z < 0 else 0) + (32 if y < 0 else 0)
             cot_in[source, x * 128 + lane - 128] = 1
+            cot_in[source, x * 128 + lane - 64] = 1
     sides = np.zeros((8, 256), np.float32)
     for (y, z), lane in wide.items():
         sides[:4, lane] = (y < 0, y >= 16, z < 0, z >= 8)
@@ -201,7 +205,7 @@
     rows32, lraw, y_send, z_send, c_send, y_recv, z_recv, c_recv, edge_a, edge_b, early,
     x4, x4i, pre1, weights1, forward2, backward2, k1s,
     p2, b2i, b2r, t2i, t2r, spread_i, spread_r, pooled, pg, gshift, bg, t3, g1,
-    total, core_in, xy_in, z_in, final, first_part, first_in, first_xy, first_z, first_final,
+    total, core_in, xy_out, xy_in, z_in, final, first_part, first_in, first_xy, first_z, first_final,
     local_sem, send_sem, recv_sem,
 ):
     dp, g, s = lax.axis_index("dp"), lax.axis_index("gx"), lax.axis_index("yz")
@@ -308,6 +312,7 @@
     far = pl.multiple_of(g * (17 * 64), 64)
     pg[pl.ds(far, 64), :] = jnp.zeros((64, 256), BF16)
     gshift[...] = jnp.zeros_like(gshift)
+    total[432:512, :] = jnp.zeros((80, 128), F32)
     early_edge.wait_recv()
     first_core = jnp.where(g == 0, jnp.float32(1.0), jnp.float32(0.0))
     half_row = lax.broadcasted_iota(jnp.int32, (8, 1), 0)
@@ -360,6 +365,23 @@
         fill_inner(j)
     for j in (1, 2):
         fill_corner(j)
+
+    zs, ys, cs = [], [], []
+    for j in range(2):
+        low, high = z_recv[0, 160:192].astype(F32), z_recv[1, 160:192].astype(F32)
+        zs.append(jnp.where(lane >= 64, unstrip(low, 64, 64, j), unstrip(high, 0, 64, j)))
+    late = lane % 4 == 3
+    for j in range(4):
+        low, high = y_recv[0, 80:96].astype(F32), y_recv[1, 80:96].astype(F32)
+        ys.append(jnp.where(lane >= 32, unstrip(low, 32, 32, j), unstrip(high, 0, 32, j)))
+        ends = [unstrip(c_recv[k, 32:48].astype(F32), 32 if k < 2 else 0, 32, j) for k in range(4)]
+        cs.append(
+            jnp.where(lane >= 32, jnp.where(late, ends[0], ends[1]), jnp.where(late, ends[2], ends[3]))
+        )
+    zs, ys, cs = (jnp.concatenate(parts, axis=0) for parts in (zs, ys, cs))
+    rim = jnp.concatenate([zs, ys, cs], axis=1).astype(BF16)
+    spread_r[...] = mm(rim, cot_in[...])
+
     copy.wait_recv()
     lraw[128:144, 512:1280] = beyond(edge_b[...])
 
@@ -410,46 +432,26 @@
     for x in range(1, 15):
         first_layer(x)
 
-    zs, ys, cs = [], [], []
-    for j in range(2):
-        low, high = z_recv[0, 160:192].astype(F32), z_recv[1, 160:192].astype(F32)
-        zs.append(jnp.where(lane >= 64, unstrip(low, 64, 64, j), unstrip(high, 0, 64, j)))
-    late = lane % 4 == 3
-    for j in range(4):
-        low, high = y_recv[0, 80:96].astype(F32), y_recv[1, 80:96].astype(F32)
-        ys.append(jnp.where(lane >= 32, unstrip(low, 32, 32, j), unstrip(high, 0, 32, j)))
-        ends = [unstrip(c_recv[k, 32:48].astype(F32), 32 if k < 2 else 0, 32, j) for k in range(4)]
-        cs.append(
-            jnp.where(lane >= 32, jnp.where(late, ends[0], ends[1]), jnp.where(late, ends[2], ends[3]))
-        )
-    zs, ys, cs = (jnp.concatenate(parts, axis=0) for parts in (zs, ys, cs))
-    rim = jnp.concatenate([zs, ys, cs], axis=1).astype(BF16)
-    spread_r[...] = mm(rim, cot_in[...])
-
     copy.wait_recv()
 
     def shift_step(tap, carry):
         got = mm(p2[...], second[tap])
         at = pl.multiple_of(tap * 32, 32)
-        for x in range(18):
-            block = got[32 * x : 32 * x + 32].astype(BF16)
-            b2i[pl.ds(at, 32), 128 * x : 128 * x + 128] = block[:, 0:128]
-            b2r[pl.ds(at, 32), 128 * x : 128 * x + 128] = block[:, 128:256]
+        for x in range(0, 18, 2):
+            one, two = got[32 * x : 32 * x + 32], got[32 * x + 32 : 32 * x + 64]
+            b2i[pl.ds(at, 32), 128 * x : 128 * x + 128] = one[:, 0:128].astype(BF16)
+            b2i[pl.ds(at, 32), 128 * x + 128 : 128 * x + 256] = two[:, 0:128].astype(BF16)
+            both = jnp.where(lane < 64, one[:, 128:256], two[:, 128:256])
+            b2r[pl.ds(at, 32), 64 * x : 64 * x + 128] = both.astype(BF16)
         return carry
 
     lax.fori_loop(0, 9, shift_step, 0, unroll=True)
 
-    def second_layer(chunk, carry):
-        at = pl.ds(pl.multiple_of(chunk * 256, 256), 256)
+    for chunk in range(9):
+        at = slice(256 * chunk, 256 * chunk + 256)
         t2i[:, at] = mm(forward2[...], b2i[:, at])
-        t2r[:, at] = mm(forward2[...], b2r[:, at])
-        return carry
-
-    lax.fori_loop(0, 9, second_layer, 0, unroll=True)
-
-    for half in (0, 7, 1, 2, 3, 4, 5, 6):
+    for half in range(8):
         lifted = spread_i[:, 128 * half : 128 * half + 128] * 0.125
-        lifted_rim = spread_r[:, 128 * half : 128 * half + 128] * 0.125
         pair = jnp.zeros((64, 128), F32)
         for x in (2 * half, 2 * half + 1):
             at = [slice(128 * (x + d), 128 * (x + d) + 128) for d in range(3)]
@@ -459,55 +461,57 @@
             pg[64 * x + 64 : 64 * x + 128, 0:128] = grad
             for d in range(3):
                 gshift[64 * d : 64 * d + 64, at[d]] = grad
-            pre = t2r[0:64, at[0]] + t2r[64:128, at[1]] + t2r[128:192, at[2]]
-            pg[64 * x + 64 : 64 * x + 128, 128:256] = (lifted_rim * slope(pre)).astype(BF16)
         high, low = split(pair)
         at = slice(128 * (half % 4), 128 * (half % 4) + 128)
         pooled[half // 4, 0:64, at] = high
         pooled[half // 4, 64:128, at] = low
-        if half == 7:
-            near_src = pl.multiple_of(jnp.where(g == 0, 16 * 64, 64), 64)
-            near_dst = pl.multiple_of(jnp.where(g == 0, 0, 17 * 64), 64)
-            copy = remote(pg.at[pl.ds(near_src, 64), :], pg.at[pl.ds(near_dst, 64), :], S_CORE + 3, other)
-            copy.start()
-            core_copies.append(copy)
-    for half in range(2):
-        sums = mm(pooled[half], pool[...])
-        feat[:, 128 * half : 128 * half + 128] = ((sums[0:64] + sums[64:128]) * 0.125).astype(BF16)
-    stores = [pltpu.make_async_copy(feat, feat_out, local_sem.at[15])]
-    stores[0].start()
 
     grad2 = mm_nt(b2i[...], gshift[...])
     total[0:288, :] = grad2[:, 0:128]
     total[288:432, 0:64] = grad2[0:144, 128:192]
     total[288:432, 64:128] = grad2[144:288, 128:192]
-    total[432:512, :] = jnp.zeros((80, 128), F32)
     mine = pl.multiple_of(g * 256, 256)
     theirs = pl.multiple_of((1 - g) * 256, 256)
     halves = remote(total.at[pl.ds(theirs, 256), :], core_in, S_CORE + 4, other)
     halves.start()
     core_copies.append(halves)
-    copy.wait_recv()
+
+    for start, end in ((0, 256), (256, 512), (512, 768), (768, 1152)):
+        t2r[:, start:end] = mm(forward2[...], b2r[:, start:end])
+    for half in (0, 7, 1, 2, 3, 4, 5, 6):
+        lifted_rim = spread_r[:, 128 * half : 128 * half + 128] * 0.125
+        here = slice(128 * half, 128 * half + 128)
+        after = slice(128 * half + 128, 128 * half + 256)
+        middle = pltpu.roll(jnp.where(lane < 64, t2r[64:128, after], t2r[64:128, here]), 64, 1)
+        rim_grad = lifted_rim * slope(t2r[0:64, here] + middle + t2r[128:192, after])
+        pg[128 * half + 64 : 128 * half + 128, 128:256] = jnp.where(lane < 64, rim_grad, 0.0).astype(BF16)
+        pg[128 * half + 128 : 128 * half + 192, 128:256] = jnp.where(lane < 64, 0.0, rim_grad).astype(BF16)
+        if half == 7:
+            near_src = pl.multiple_of(jnp.where(g == 0, 16 * 64, 64), 64)
+            near_dst = pl.multiple_of(jnp.where(g == 0, 0, 17 * 64), 64)
+            edges = remote(pg.at[pl.ds(near_src, 64), :], pg.at[pl.ds(near_dst, 64), :], S_CORE + 3, other)
+            edges.start()
+            core_copies.append(edges)
     halves.wait_recv()
+    spot = dp * 4 + yi
+    place = pl.multiple_of(spot * 16, 16)
     core_in[...] = core_in[...] + total[pl.ds(mine, 256), :]
+    xy_out[...] = core_in[...].astype(BF16)
     xy_copies = []
     for i, (a, b) in enumerate(XY):
         piece = ((dp + a) % 4) * 4 + (yi + b) % 4
-        source = core_in.at[pl.ds(pl.multiple_of(piece * 16, 16), 16), :]
+        source = xy_out.at[pl.ds(pl.multiple_of(piece * 16, 16), 16), :]
         copy = remote(source, xy_in.at[i], S_XY + i, flat[i])
         copy.start()
         xy_copies.append(copy)
-
-    def back_step(step, carry):
+    edges.wait_recv()
+
+    for step in range(5):
         got = mm(pg[...], back[step])
-        at = pl.multiple_of(step * 128, 128)
         for x in range(18):
             block = got[64 * x : 64 * x + 64].astype(BF16)
-            bg[pl.ds(at, 64), 128 * x : 128 * x + 128] = block[:, 0:128]
-            bg[pl.ds(at + 64, 64), 128 * x : 128 * x + 128] = block[:, 128:256]
-        return carry
-
-    lax.fori_loop(0, 5, back_step, 0, unroll=True)
+            bg[128 * step : 128 * step + 64, 128 * x : 128 * x + 128] = block[:, 0:128]
+            bg[128 * step + 64 : 128 * step + 128, 128 * x : 128 * x + 128] = block[:, 128:256]
 
     def back_layer(chunk, carry):
         at = pl.ds(pl.multiple_of(chunk * 256, 256), 256)
@@ -527,8 +531,8 @@
         for phase in range(8):
             at = slice(32 * phase, 32 * phase + 32)
             g1[at, 128 * x : 128 * x + 128] = (eighth * slope(pre1[x, at, :])).astype(BF16)
-    stores.append(pltpu.make_async_copy(grads, grad_out, local_sem.at[16]))
-    stores[1].start()
+    stores = [pltpu.make_async_copy(grads, grad_out, local_sem.at[16])]
+    stores[0].start()
     wide = mm_nt(g1[...], x4i[...])
     partial = jnp.zeros((64, 128), F32)
     for phase in range(8):
@@ -541,10 +545,8 @@
     swap = remote(first_part.at[pl.ds(their_half, 16), :], first_in, S_CORE + 5, other)
     swap.start()
     core_copies.append(swap)
-    spot = dp * 4 + yi
-    place = pl.multiple_of(spot * 16, 16)
     swap.wait_recv()
-    first_xy[spot] = first_in[...] + first_part[pl.ds(my_half, 16), :]
+    first_xy[spot] = (first_in[...] + first_part[pl.ds(my_half, 16), :]).astype(BF16)
     fxy_copies = []
     for i in range(15):
         copy = remote(first_xy.at[spot], first_xy.at[spot], S_FXY + i, flat[i])
@@ -552,11 +554,16 @@
         fxy_copies.append(copy)
     for sent in rim_copies + core_copies[:5]:
         sent.wait_send()
+    for half in range(2):
+        sums = mm(pooled[half], pool[...])
+        feat[:, 128 * half : 128 * half + 128] = ((sums[0:64] + sums[64:128]) * 0.125).astype(BF16)
+    stores.append(pltpu.make_async_copy(feat, feat_out, local_sem.at[15]))
+    stores[1].start()
     part = core_in[pl.ds(place, 16), :]
     for i, copy in enumerate(xy_copies):
         copy.wait_recv()
-        part = part + xy_in[i]
-    z_in[zi] = part
+        part = part + xy_in[i].astype(F32)
+    z_in[zi] = part.astype(BF16)
     z_copies = []
     for k in range(7):
         copy = remote(z_in.at[zi], z_in.at[zi], S_Z + k, tall[k])
@@ -564,10 +571,10 @@
         z_copies.append(copy)
     for copy in fxy_copies:
         copy.wait_recv()
-    part = first_xy[0]
+    part = first_xy[0].astype(F32)
     for k in range(1, 16):
-        part = part + first_xy[k]
-    first_z[zi] = part
+        part = part + first_xy[k].astype(F32)
+    first_z[zi] = part.astype(BF16)
     fz_copies = []
     for k in range(7):
         copy = remote(first_z.at[zi], first_z.at[zi], S_FZ + k, tall[k])
@@ -575,11 +582,11 @@
         fz_copies.append(copy)
     for copy in z_copies:
         copy.wait_recv()
-    part = z_in[0]
+    part = z_in[0].astype(F32)
     for k in range(1, 8):
-        part = part + z_in[k]
+        part = part + z_in[k].astype(F32)
     rows = pl.ds(pl.multiple_of(mine + place, 16), 16)
-    final[rows, :] = part
+    final[rows, :] = part.astype(BF16)
     ag_copies = []
     for i in range(15):
         copy = remote(final.at[rows, :], final.at[rows, :], S_AG + i, flat[i])
@@ -595,9 +602,9 @@
     core_copies.append(joined)
     for copy in fz_copies:
         copy.wait_recv()
-    part = first_z[0]
+    part = first_z[0].astype(F32)
     for k in range(1, 8):
-        part = part + first_z[k]
+        part = part + first_z[k].astype(F32)
     half = pl.ds(my_half, 16)
     first_final[half, :] = part
     copy = remote(first_final.at[half, :], first_final.at[half, :], S_CORE + 7, other)
@@ -623,12 +630,12 @@
     grad_out[...] = grad[...]
     for a in range(9):
         at = slice(32 * a, 32 * a + 32)
-        second_out[a] = second[at, 0:64]
-        second_out[9 + a] = second[at, 64:128]
-    for a in range(36):
-        row = 288 + (8 * a) % 144
-        lanes = slice(0, 64) if a < 18 else slice(64, 128)
-        second_out[18 + a // 4, 8 * (a % 4) : 8 * (a % 4) + 8, :] = second[row : row + 8, lanes]
+        second_out[a] = second[at, 0:64].astype(F32)
+        second_out[9 + a] = second[at, 64:128].astype(F32)
+    for a in range(18):
+        row = 288 + (16 * a) % 144
+        lanes = slice(0, 64) if a < 9 else slice(64, 128)
+        second_out[18 + a // 2, 16 * (a % 2) : 16 * (a % 2) + 16, :] = second[row : row + 16, lanes].astype(F32)
     flipped = first[...].T
     for tap in range(27):
         first_out[tap] = flipped[4 * tap : 4 * tap + 4, :]
@@ -649,12 +656,12 @@
         vmem((16, 512), BF16), vmem((16, 768), BF16), vmem((8, 144, 256), F32),
         vmem((16, 256, 256), BF16), vmem((256, 2048), BF16), vmem((16, 256, 128), F32),
         vmem((256, 256), BF16), vmem((192, 288), BF16), vmem((96, 576), BF16), vmem((128, 32), F32),
-        vmem((576, 256), BF16), vmem((288, 2304), BF16), vmem((288, 2304), BF16),
-        vmem((192, 2304), F32), vmem((192, 2304), F32), vmem((64, 1024), F32), vmem((64, 1024), F32),
+        vmem((576, 256), BF16), vmem((288, 2304), BF16), vmem((288, 1152), BF16),
+        vmem((192, 2304), F32), vmem((192, 1152), F32), vmem((64, 1024), F32), vmem((64, 1024), F32),
         vmem((2, 128, 512), BF16), vmem((1152, 256), BF16), vmem((192, 2304), BF16),
         vmem((640, 2304), BF16), vmem((96, 2304), F32), vmem((256, 2048), BF16),
-        vmem((512, 128), F32), vmem((256, 128), F32), vmem((15, 16, 128), F32), vmem((8, 16, 128), F32), vmem((512, 128), F32),
-        vmem((32, 128), F32), vmem((16, 128), F32), vmem((16, 16, 128), F32), vmem((8, 16, 128), F32), vmem((32, 128), F32),
+        vmem((512, 128), F32), vmem((256, 128), F32), vmem((256, 128), BF16), vmem((15, 16, 128), BF16), vmem((8, 16, 128), BF16), vmem((512, 128), BF16),
+        vmem((32, 128), F32), vmem((16, 128), F32), vmem((16, 16, 128), BF16), vmem((8, 16, 128), BF16), vmem((32, 128), F32),
         pltpu.SemaphoreType.DMA((19,)), pltpu.SemaphoreType.DMA((75,)), pltpu.SemaphoreType.DMA((75,)),
     ]
     parts = pl.pallas_call(
@@ -662,7 +669,7 @@
         out_shape=(
             jax.ShapeDtypeStruct((64, 256), BF16),
             jax.ShapeDtypeStruct((512, 128), F32),
-            jax.ShapeDtypeStruct((432, 128), F32),
+            jax.ShapeDtypeStruct((432, 128), BF16),
             jax.ShapeDtypeStruct((32, 128), F32),
         ),
         in_specs=[there] * 15,

time: 45 us -> 43.5 us (0.967)
  Pallas kernels: 44.3 us -> 42.7 us
    pallas_call x1, Pallas kernels: 42.3 us -> 40.8 us  [on_device(): pl.pallas_call(body, out_shape=(jax.ShapeDtypeStruct((64, 256), BF16), ja...]
where the time goes in v5:
time: 43.5 us; the launch traced here: 43.4 us
  Pallas kernels  42.7 us (98%)
  between operations  0.64 us (1%)
    pallas_call x1, Pallas kernels, on_device(): pl.pallas_call(body, out_shape=(jax.ShapeDtypeStruct((64, 256), BF16), ja...  40.8 us
    pallas_call x1, Pallas kernels, on_device(): pl.pallas_call(arrange, out_shape=(jax.ShapeDtypeStruct((64, 256), BF16),...  1.95 us

profile of v5, /device:TPU:1, one launch (start us, length us, event | category | flops | bytes accessed | tf_op | source)
XLA Modules:
  0.0 43.4 jit_solution(3184821873493373902)
XLA Ops:
  0.6 40.8 %shard_map.174 = (bf16[64,256]{1,0:T(8,128)(2,1)}, f32[512,128]{1,0:T(8,128)}, bf16[432,128]{1,0:T(8,128)(2,1)}, f32[32,128]{1,0:T(8,128)}) custom-call(bf16[4,16384]{1,0:T(4,128)(2,1)} %bitcast.17, bf16[27,4,32]{2,1,0:T(4,128)(2,1)} %bitcast.19, bf16[27,32,64]{2,1,0:T(8,128)(2,1)} %bitcast.16, bf16[64,256]{1,0:T(8,128)(2,1)} %bitcast.18, ...), custom_call_target="tpu_custom_call" | custom-call | tf_op jit(solution)/shard_map/pallas_call | solution.py:667
  41.4 1.9 %shard_map.175 = (bf16[64,256]{1,0:T(8,128)(2,1)}, f32[512,128]{1,0:T(8,128)}, f32[27,4,32]{2,1,0:T(4,128)}, f32[27,32,64]{2,1,0:T(8,128)}) custom-call(bf16[64,256]{1,0:T(8,128)(2,1)} %get-tuple-element.12.feat, f32[512,128]{1,0:T(8,128)} %get-tuple-element.13.grad, bf16[432,128]{1,0:T(8,128)(2,1)} %get-tuple-element.14.second, ...), custom_call_target="tpu_custom_call" | custom-call | tf_op jit(solution)/shard_map/pallas_call | solution.py:688

commit v6 on v5

--- a/solution.py
+++ b/solution.py
@@ -552,13 +552,6 @@
         copy = remote(first_xy.at[spot], first_xy.at[spot], S_FXY + i, flat[i])
         copy.start()
         fxy_copies.append(copy)
-    for sent in rim_copies + core_copies[:5]:
-        sent.wait_send()
-    for half in range(2):
-        sums = mm(pooled[half], pool[...])
-        feat[:, 128 * half : 128 * half + 128] = ((sums[0:64] + sums[64:128]) * 0.125).astype(BF16)
-    stores.append(pltpu.make_async_copy(feat, feat_out, local_sem.at[15]))
-    stores[1].start()
     part = core_in[pl.ds(place, 16), :]
     for i, copy in enumerate(xy_copies):
         copy.wait_recv()
@@ -569,6 +562,13 @@
         copy = remote(z_in.at[zi], z_in.at[zi], S_Z + k, tall[k])
         copy.start()
         z_copies.append(copy)
+    for sent in rim_copies + core_copies[:5]:
+        sent.wait_send()
+    for half in range(2):
+        sums = mm(pooled[half], pool[...])
+        feat[:, 128 * half : 128 * half + 128] = ((sums[0:64] + sums[64:128]) * 0.125).astype(BF16)
+    stores.append(pltpu.make_async_copy(feat, feat_out, local_sem.at[15]))
+    stores[1].start()
     for copy in fxy_copies:
         copy.wait_recv()
     part = first_xy[0].astype(F32)

time: 43.5 us -> 43.2 us (level)
  no operation moved by 1% of the time
where the time goes in v6:
time: 43.2 us; the launch traced here: 43.1 us
  Pallas kernels  42.5 us (98%)
  between operations  0.64 us (1%)
    pallas_call x1, Pallas kernels, on_device(): pl.pallas_call(body, out_shape=(jax.ShapeDtypeStruct((64, 256), BF16), ja...  40.5 us
    pallas_call x1, Pallas kernels, on_device(): pl.pallas_call(arrange, out_shape=(jax.ShapeDtypeStruct((64, 256), BF16),...  1.95 us

profile of v6, /device:TPU:1, one launch (start us, length us, event | category | flops | bytes accessed | tf_op | source)
XLA Modules:
  0.0 43.1 jit_solution(6965572304373668075)
XLA Ops:
  0.6 40.5 %shard_map.174 = (bf16[64,256]{1,0:T(8,128)(2,1)}, f32[512,128]{1,0:T(8,128)}, bf16[432,128]{1,0:T(8,128)(2,1)}, f32[32,128]{1,0:T(8,128)}) custom-call(bf16[4,16384]{1,0:T(4,128)(2,1)} %bitcast.17, bf16[27,4,32]{2,1,0:T(4,128)(2,1)} %bitcast.19, bf16[27,32,64]{2,1,0:T(8,128)(2,1)} %bitcast.16, bf16[64,256]{1,0:T(8,128)(2,1)} %bitcast.18, ...), custom_call_target="tpu_custom_call" | custom-call | tf_op jit(solution)/shard_map/pallas_call | solution.py:667
  41.2 1.9 %shard_map.175 = (bf16[64,256]{1,0:T(8,128)(2,1)}, f32[512,128]{1,0:T(8,128)}, f32[27,4,32]{2,1,0:T(4,128)}, f32[27,32,64]{2,1,0:T(8,128)}) custom-call(bf16[64,256]{1,0:T(8,128)(2,1)} %get-tuple-element.12.feat, f32[512,128]{1,0:T(8,128)} %get-tuple-element.13.grad, bf16[432,128]{1,0:T(8,128)(2,1)} %get-tuple-element.14.second, ...), custom_call_target="tpu_custom_call" | custom-call | tf_op jit(solution)/shard_map/pallas_call | solution.py:688
